TPU v7x, 128 devices: a whole 4x4x4 slice. The times are simulated.
128 devices in a mesh: layer: 2 (over core), gy: 8 (over y_lo, z), gx: 8 (over x, y_hi).
Axes of the slice: x: 4, y: 4 (y_hi: 2, y_lo: 2; y = y_hi * 2 + y_lo), z: 4, core: 2. Of those that a mesh axis runs over, the one named last changes fastest.
Arguments:
- frames: bfloat16 [2, 32, 2048, 256], P(None, 'gy', 'gx'), may hold values from -6 to 6
- hidden_init: bfloat16 [2, 32, 2048, 256], P('layer', 'gy', 'gx'), may hold values from -1 to 1
- cell_init: float32 [2, 32, 2048, 256], P('layer', 'gy', 'gx'), may hold values from -5 to 5
- conv_weight: bfloat16 [2, 4608, 1024], P('layer'), may hold values from -0.09375 to 0.09375
- conv_bias: float32 [2, 1024], replicated, may hold values from -4 to 4
Outputs:
- hidden_out: bfloat16 [2, 32, 2048, 256], P('layer', 'gy', 'gx')
- cell_out: float32 [2, 32, 2048, 256], P('layer', 'gy', 'gx')
All inputs are finite; a program needn't handle non-finite values.
Results may differ from a plain program's by a relative error of at most 0.0021.
Values may be sent and summed in bfloat16 or wider, within the bound.
No kernel may reach another device: no remote copies, remote signals or barrier semaphores. Data moves between devices by JAX's collectives and lax.ppermute only.
A program may use at most 128 MiB of HBM per device.

v0:
```python
import jax
import jax.numpy as jnp
from jax import lax
from jax.sharding import PartitionSpec as P


def passed_along(value, axis, steps):
    count = lax.axis_size(axis)
    leading, last = (max(0, -steps), min(count, count - steps))
    return lax.ppermute(value, axis, [(source, source + steps) for source in range(leading, last)])


def extended(block, sides, width):
    for axis, dim in sides:
        count = lax.axis_size(axis)
        forward = [(i, i + 1) for i in range(count - 1)]
        backward = [(target, source) for source, target in forward]
        low = lax.ppermute(
            lax.slice_in_dim(block, block.shape[dim] - width, None, axis=dim), axis, forward
        )
        high = lax.ppermute(lax.slice_in_dim(block, 0, width, axis=dim), axis, backward)
        block = jnp.concatenate([low, block, high], axis=dim)
    return block


def tile_gates(padded, kernel, rows, cols):
    width = padded.shape[-1]
    total = jnp.zeros((rows * cols, kernel.shape[1]), jnp.float32)
    for tap in range(9):
        window = padded[tap // 3 : tap // 3 + rows, tap % 3 : tap % 3 + cols, :].reshape(-1, width)
        total = total + jnp.dot(
            window, kernel[tap * width : (tap + 1) * width], preferred_element_type=jnp.float32
        )
    return total


def cell_update(gates, cell):
    chan = cell.shape[-1]
    gates = gates.reshape(cell.shape[0], cell.shape[1], 4 * chan)
    in_gate = jax.nn.sigmoid(gates[..., :chan])
    forget = jax.nn.sigmoid(gates[..., chan : 2 * chan])
    out_gate = jax.nn.sigmoid(gates[..., 2 * chan : 3 * chan])
    candidate = jnp.tanh(gates[..., 3 * chan :])
    new_cell = forget * cell + in_gate * candidate
    new_hidden = (out_gate * jnp.tanh(new_cell)).astype(jnp.bfloat16)
    return (new_cell, new_hidden)


def per_device(frames, hidden_init, cell_init, conv_weight, conv_bias):
    section = lax.axis_index("layer")
    n_frames = frames.shape[0]
    rows = frames.shape[1]
    cols = frames.shape[2]
    kernel = conv_weight[0]
    bias = lax.dynamic_index_in_dim(conv_bias, section, 0, keepdims=False)
    hidden = hidden_init[0]
    cell = cell_init[0]
    for step in range(n_frames + 1):
        if step == 0:
            received = jnp.zeros_like(hidden)
        else:
            received = passed_along(hidden, "layer", 1)
        source = jnp.where(section == 0, frames[min(step, n_frames - 1)], received)
        joined = jnp.concatenate([source, hidden], axis=-1)
        padded = extended(joined, (("gy", 0), ("gx", 1)), 1)
        gates = tile_gates(padded, kernel, rows, cols) + bias[None, :]
        new_cell, new_hidden = cell_update(gates, cell)
        active = jnp.logical_and(step - section >= 0, step - section < n_frames)
        cell = jnp.where(active, new_cell, cell)
        hidden = jnp.where(active, new_hidden, hidden)
    return (hidden[None], cell[None])


def solution(mesh):
    placed = (
        P(None, "gy", "gx", None),
        P("layer", "gy", "gx", None),
        P("layer", "gy", "gx", None),
        P("layer", None, None),
        P(),
    )
    return jax.shard_map(
        per_device,
        mesh=mesh,
        in_specs=placed,
        out_specs=(P("layer", "gy", "gx", None), P("layer", "gy", "gx", None)),
        check_vma=False,
    )
```

profile of v0, /device:TPU:1, one launch (start us, length us, event | category | flops | bytes accessed | tf_op | source)
XLA Modules:
  0.0 198.3 jit_solution(4523426814858783835)
XLA Ops:
  2.7 4.4 %collective-permute-start = (bf16[1,256,512]{2,1,0:T(8,128)(2,1)S(1)}, bf16[1,256,512]{2,1,0:T(8,128)(2,1)S(1)}, u32[]{:S(2)}, u32[]{:S(2)}) collective-permute-start(bf16[1,256,512]{2,1,0:T(8,128)(2,1)S(1)} %get-tuple-element.51), channel_id=1, source_target_pairs={{0,8},{8,16},{16,24},{24,32},{32,40},{40,48},{48,56},{1,9},{9,17},... | collective-permute-start | bytes 786440 | tf_op jit(solution)/shard_map/ppermute | solution.py:18
  12.4 3.9 %collective-permute-done.1 = bf16[1,256,512]{2,1,0:T(8,128)(2,1)S(1)} collective-permute-done((bf16[1,256,512]{2,1,0:T(8,128)(2,1)S(1)}, bf16[1,256,512]{2,1,0:T(8,128)(2,1)S(1)}, u32[]{:S(2)}, u32[]{:S(2)}) %collective-permute-start.1) | collective-permute-done | bytes 262176 | tf_op jit(solution)/shard_map/ppermute | solution.py:21
  17.6 5.5 %collective-permute-start.2 = (bf16[6,1,512]{2,1,0:T(2,128)(2,1)S(1)}, bf16[6,1,512]{2,1,0:T(2,128)(2,1)S(1)}, u32[]{:S(2)}, u32[]{:S(2)}) collective-permute-start(bf16[6,1,512]{2,1,0:T(2,128)(2,1)S(1)} %get-tuple-element.38), channel_id=1, source_target_pairs={{0,1},{1,2},{2,3},{3,4},{4,5},{5,6},{6,7},{8,9},{9,10},{10,11},{11... | collective-permute-start | bytes 18440 | tf_op jit(solution)/shard_map/ppermute | solution.py:18
  23.3 3.2 %fusion.59 = f32[1024,1024]{1,0:T(8,128)} fusion(bf16[1024,512]{1,0:T(8,128)(2,1)S(1)} %bitcast.165, bf16[1,4608,1024]{2,1,0:T(8,128)(2,1)S(1)} %copy-done.7), kind=kOutput, calls=%fused_computation.97 | convolution fusion | flops 1073741824 | bytes 6291456 | tf_op jit(solution)/shard_map/dot_general | solution.py:31
  26.5 3.3 %fusion.94 = f32[1024,1024]{1,0:T(8,128)} fusion(bf16[1024,512]{1,0:T(8,128)(2,1)S(1)} %bitcast.164, bf16[1,4608,1024]{2,1,0:T(8,128)(2,1)S(1)} %copy-done.7), kind=kOutput, calls=%fused_computation.132 | convolution fusion | flops 1073741824 | bytes 6291456 | tf_op jit(solution)/shard_map/dot_general | solution.py:31
  32.0 3.3 %fusion.71 = f32[1024,1024]{1,0:T(8,128)} fusion(bf16[1024,512]{1,0:T(8,128)(2,1)S(1)} %bitcast.163, bf16[1,4608,1024]{2,1,0:T(8,128)(2,1)S(1)} %copy-done.7), kind=kOutput, calls=%fused_computation.109 | convolution fusion | flops 1073741824 | bytes 6291456 | tf_op jit(solution)/shard_map/dot_general | solution.py:31
  35.4 3.3 %fusion.65 = f32[1024,1024]{1,0:T(8,128)} fusion(bf16[1024,512]{1,0:T(8,128)(2,1)S(1)} %bitcast.162, bf16[1,4608,1024]{2,1,0:T(8,128)(2,1)S(1)} %copy-done.7), kind=kOutput, calls=%fused_computation.103 | convolution fusion | flops 1073741824 | bytes 6291456 | tf_op jit(solution)/shard_map/dot_general | solution.py:31
  41.8 3.2 %fusion.88 = f32[1024,1024]{1,0:T(8,128)} fusion(bf16[1024,512]{1,0:T(8,128)(2,1)S(1)} %bitcast.160, bf16[1,4608,1024]{2,1,0:T(8,128)(2,1)S(1)} %copy-done.7), kind=kOutput, calls=%fused_computation.126 | convolution fusion | flops 1073741824 | bytes 6291456 | tf_op jit(solution)/shard_map/dot_general | solution.py:31
  45.0 3.3 %fusion.100 = f32[1024,1024]{1,0:T(8,128)} fusion(bf16[1024,512]{1,0:T(8,128)(2,1)S(1)} %bitcast.159, bf16[1,4608,1024]{2,1,0:T(8,128)(2,1)S(1)} %copy-done.7), kind=kOutput, calls=%fused_computation.138 | convolution fusion | flops 1073741824 | bytes 6291456 | tf_op jit(solution)/shard_map/dot_general | solution.py:31
  48.3 10.1 %add_add_fusion.2 = f32[1024,1024]{1,0:T(8,128)S(1)} fusion(f32[1024,1024]{1,0:T(8,128)S(1)} %copy-done.3, f32[1024,1024]{1,0:T(8,128)} %fusion.65, f32[1024,1024]{1,0:T(8,128)} %fusion.71, f32[1024,1024]{1,0:T(8,128)S(1)} %fusion.39, f32[1024,1024]{1,0:T(8,128)} %fusion.82, f32[1024,1024]{1,0:T(8,128)} %fusion.88, f32[1024,1024]{1,0:T(8,128)} %fusion.100, ...), kind=kOutput, calls=%fused_computation.2 | convolution fusion | flops 1083179008 | bytes 39849984 | tf_op jit(solution)/shard_map/dot_general | solution.py:31
  61.8 3.6 %collective-permute-done.4 = bf16[4,256,256]{2,1,0:T(8,128)(2,1)S(1)} collective-permute-done((bf16[4,256,256]{2,1,0:T(8,128)(2,1)S(1)}, bf16[4,256,256]{2,1,0:T(8,128)(2,1)S(1)}, u32[]{:S(2)}, u32[]{:S(2)}) %collective-permute-start.4) | collective-permute-done | bytes 524320 | tf_op jit(solution)/shard_map/ppermute | solution.py:10
  65.6 3.4 %collective-permute-start.5 = (bf16[1,256,512]{2,1,0:T(8,128)(2,1)S(1)}, bf16[1,256,512]{2,1,0:T(8,128)(2,1)S(1)}, u32[]{:S(2)}, u32[]{:S(2)}) collective-permute-start(bf16[1,256,512]{2,1,0:T(8,128)(2,1)S(1)} %get-tuple-element.47), channel_id=1, source_target_pairs={{0,8},{8,16},{16,24},{24,32},{32,40},{40,48},{48,56},{1,9},{9,17},... | collective-permute-start | bytes 786440 | tf_op jit(solution)/shard_map/ppermute | solution.py:18
  70.4 4.1 %collective-permute-done.5 = bf16[1,256,512]{2,1,0:T(8,128)(2,1)S(1)} collective-permute-done((bf16[1,256,512]{2,1,0:T(8,128)(2,1)S(1)}, bf16[1,256,512]{2,1,0:T(8,128)(2,1)S(1)}, u32[]{:S(2)}, u32[]{:S(2)}) %collective-permute-start.5) | collective-permute-done | bytes 262176 | tf_op jit(solution)/shard_map/ppermute | solution.py:18
  74.5 3.8 %collective-permute-done.6 = bf16[1,256,512]{2,1,0:T(8,128)(2,1)S(1)} collective-permute-done((bf16[1,256,512]{2,1,0:T(8,128)(2,1)S(1)}, bf16[1,256,512]{2,1,0:T(8,128)(2,1)S(1)}, u32[]{:S(2)}, u32[]{:S(2)}) %collective-permute-start.6) | collective-permute-done | bytes 262176 | tf_op jit(solution)/shard_map/ppermute | solution.py:21
  79.6 6.4 %collective-permute-start.7 = (bf16[6,1,512]{2,1,0:T(2,128)(2,1)S(1)}, bf16[6,1,512]{2,1,0:T(2,128)(2,1)S(1)}, u32[]{:S(2)}, u32[]{:S(2)}) collective-permute-start(bf16[6,1,512]{2,1,0:T(2,128)(2,1)S(1)} %get-tuple-element.34), channel_id=1, source_target_pairs={{0,1},{1,2},{2,3},{3,4},{4,5},{5,6},{6,7},{8,9},{9,10},{10,11},{11... | collective-permute-start | bytes 18440 | tf_op jit(solution)/shard_map/ppermute | solution.py:18
  91.6 3.3 %fusion.75 = f32[1024,1024]{1,0:T(8,128)} fusion(bf16[1024,512]{1,0:T(8,128)(2,1)S(1)} %bitcast.170, bf16[1,4608,1024]{2,1,0:T(8,128)(2,1)S(1)} %bitcast.156), kind=kOutput, calls=%fused_computation.113 | convolution fusion | flops 1073741824 | bytes 6291456 | tf_op jit(solution)/shard_map/dot_general | solution.py:31
  96.7 3.3 %fusion.69 = f32[1024,1024]{1,0:T(8,128)} fusion(bf16[1024,512]{1,0:T(8,128)(2,1)S(1)} %bitcast.175, bf16[1,4608,1024]{2,1,0:T(8,128)(2,1)S(1)} %bitcast.156), kind=kOutput, calls=%fused_computation.107 | convolution fusion | flops 1073741824 | bytes 6291456 | tf_op jit(solution)/shard_map/dot_general | solution.py:31
  100.3 3.2 %fusion.63 = f32[1024,1024]{1,0:T(8,128)} fusion(bf16[1024,512]{1,0:T(8,128)(2,1)S(1)} %bitcast.176, bf16[1,4608,1024]{2,1,0:T(8,128)(2,1)S(1)} %bitcast.156), kind=kOutput, calls=%fused_computation.101 | convolution fusion | flops 1073741824 | bytes 6291456 | tf_op jit(solution)/shard_map/dot_general | solution.py:31
  103.5 3.3 %fusion.98 = f32[1024,1024]{1,0:T(8,128)} fusion(bf16[1024,512]{1,0:T(8,128)(2,1)S(1)} %bitcast.171, bf16[1,4608,1024]{2,1,0:T(8,128)(2,1)S(1)} %bitcast.156), kind=kOutput, calls=%fused_computation.136 | convolution fusion | flops 1073741824 | bytes 6291456 | tf_op jit(solution)/shard_map/dot_general | solution.py:31
  110.0 3.2 %fusion.86 = f32[1024,1024]{1,0:T(8,128)} fusion(bf16[1024,512]{1,0:T(8,128)(2,1)S(1)} %bitcast.166, bf16[1,4608,1024]{2,1,0:T(8,128)(2,1)S(1)} %bitcast.156), kind=kOutput, calls=%fused_computation.124 | convolution fusion | flops 1073741824 | bytes 6291456 | tf_op jit(solution)/shard_map/dot_general | solution.py:31
  113.2 10.0 %add_add_fusion.1 = f32[1024,1024]{1,0:T(8,128)S(1)} fusion(f32[1024,1024]{1,0:T(8,128)S(1)} %fusion.57, f32[1024,1024]{1,0:T(8,128)} %fusion.63, f32[1024,1024]{1,0:T(8,128)} %fusion.69, f32[1024,1024]{1,0:T(8,128)} %fusion.75, f32[1024,1024]{1,0:T(8,128)} %fusion.80, f32[1024,1024]{1,0:T(8,128)} %fusion.86, f32[1024,1024]{1,0:T(8,128)} %fusion.98, ...), kind=kOutput, calls=%fused_computation.1 | convolution fusion | flops 1083179008 | bytes 39849984 | tf_op jit(solution)/shard_map/dot_general | solution.py:31
  127.0 3.2 %collective-permute-done.9 = bf16[4,256,256]{2,1,0:T(8,128)(2,1)S(1)} collective-permute-done((bf16[4,256,256]{2,1,0:T(8,128)(2,1)S(1)}, bf16[4,256,256]{2,1,0:T(8,128)(2,1)S(1)}, u32[]{:S(2)}, u32[]{:S(2)}) %collective-permute-start.9) | collective-permute-done | bytes 524320 | tf_op jit(solution)/shard_map/ppermute | solution.py:10
  131.1 3.9 %collective-permute-start.10 = (bf16[1,256,512]{2,1,0:T(8,128)(2,1)}, bf16[1,256,512]{2,1,0:T(8,128)(2,1)S(1)}, u32[]{:S(2)}, u32[]{:S(2)}) collective-permute-start(bf16[1,256,512]{2,1,0:T(8,128)(2,1)} %get-tuple-element.42), channel_id=1, source_target_pairs={{0,8},{8,16},{16,24},{24,32},{32,40},{40,48},{48,56},{1,9},{9,17},... | collective-permute-start | bytes 786440 | tf_op jit(solution)/shard_map/ppermute | solution.py:18
  136.4 4.5 %collective-permute-done.10 = bf16[1,256,512]{2,1,0:T(8,128)(2,1)S(1)} collective-permute-done((bf16[1,256,512]{2,1,0:T(8,128)(2,1)}, bf16[1,256,512]{2,1,0:T(8,128)(2,1)S(1)}, u32[]{:S(2)}, u32[]{:S(2)}) %collective-permute-start.10) | collective-permute-done | bytes 262176 | tf_op jit(solution)/shard_map/ppermute | solution.py:18
  140.9 3.8 %collective-permute-done.11 = bf16[1,256,512]{2,1,0:T(8,128)(2,1)} collective-permute-done((bf16[1,256,512]{2,1,0:T(8,128)(2,1)}, bf16[1,256,512]{2,1,0:T(8,128)(2,1)}, u32[]{:S(2)}, u32[]{:S(2)}) %collective-permute-start.11) | collective-permute-done | bytes 262176 | tf_op jit(solution)/shard_map/ppermute | solution.py:21
  146.8 6.9 %collective-permute-start.12 = (bf16[6,1,512]{2,1,0:T(2,128)(2,1)S(1)}, bf16[6,1,512]{2,1,0:T(2,128)(2,1)S(1)}, u32[]{:S(2)}, u32[]{:S(2)}) collective-permute-start(bf16[6,1,512]{2,1,0:T(2,128)(2,1)S(1)} %get-tuple-element.30), channel_id=1, source_target_pairs={{0,1},{1,2},{2,3},{3,4},{4,5},{5,6},{6,7},{8,9},{9,10},{10,11},{11... | collective-permute-start | bytes 18440 | tf_op jit(solution)/shard_map/ppermute | solution.py:18
  160.2 3.2 %fusion.73 = f32[1024,1024]{1,0:T(8,128)} fusion(bf16[1024,512]{1,0:T(8,128)(2,1)S(1)} %bitcast.172, bf16[1,4608,1024]{2,1,0:T(8,128)(2,1)S(1)} %bitcast.158), kind=kOutput, calls=%fused_computation.111 | convolution fusion | flops 1073741824 | bytes 6291456 | tf_op jit(solution)/shard_map/dot_general | solution.py:31
  167.3 3.3 %fusion.67 = f32[1024,1024]{1,0:T(8,128)} fusion(bf16[1024,512]{1,0:T(8,128)(2,1)S(1)} %bitcast.178, bf16[1,4608,1024]{2,1,0:T(8,128)(2,1)S(1)} %bitcast.158), kind=kOutput, calls=%fused_computation.105 | convolution fusion | flops 1073741824 | bytes 6291456 | tf_op jit(solution)/shard_map/dot_general | solution.py:31
  170.9 3.3 %fusion.61 = f32[1024,1024]{1,0:T(8,128)} fusion(bf16[1024,512]{1,0:T(8,128)(2,1)S(1)} %bitcast.179, bf16[1,4608,1024]{2,1,0:T(8,128)(2,1)S(1)} %bitcast.158), kind=kOutput, calls=%fused_computation.99 | convolution fusion | flops 1073741824 | bytes 6291456 | tf_op jit(solution)/shard_map/dot_general | solution.py:31
  174.2 3.3 %fusion.96 = f32[1024,1024]{1,0:T(8,128)} fusion(bf16[1024,512]{1,0:T(8,128)(2,1)S(1)} %bitcast.173, bf16[1,4608,1024]{2,1,0:T(8,128)(2,1)S(1)} %bitcast.158), kind=kOutput, calls=%fused_computation.134 | convolution fusion | flops 1073741824 | bytes 6291456 | tf_op jit(solution)/shard_map/dot_general | solution.py:31
  180.6 3.2 %fusion.84 = f32[1024,1024]{1,0:T(8,128)} fusion(bf16[1024,512]{1,0:T(8,128)(2,1)S(1)} %bitcast.167, bf16[1,4608,1024]{2,1,0:T(8,128)(2,1)S(1)} %bitcast.158), kind=kOutput, calls=%fused_computation.122 | convolution fusion | flops 1073741824 | bytes 6291456 | tf_op jit(solution)/shard_map/dot_general | solution.py:31
  183.8 11.6 %add_add_fusion = f32[1024,1024]{1,0:T(8,128)S(1)} fusion(f32[1024,1024]{1,0:T(8,128)S(1)} %fusion.55, f32[1024,1024]{1,0:T(8,128)} %fusion.61, f32[1024,1024]{1,0:T(8,128)} %fusion.67, f32[1024,1024]{1,0:T(8,128)} %fusion.73, f32[1024,1024]{1,0:T(8,128)} %fusion.78, f32[1024,1024]{1,0:T(8,128)} %fusion.84, f32[1024,1024]{1,0:T(8,128)} %fusion.96, ...), kind=kOutput, calls=%fused_computation | convolution fusion | flops 1083179008 | bytes 39849984 | tf_op jit(solution)/shard_map/dot_general | solution.py:31
  (79 shorter events, 55.9 us)
Async XLA Ops:
  0.6 8.9 %copy-start = (f32[2,1024]{1,0:T(2,128)S(1)}, f32[2,1024]{1,0:T(2,128)}, u32[]{:S(2)}) copy-start(f32[2,1024]{1,0:T(2,128)} %param.9) | copy-start | bytes 24580
  2.7 9.6 %collective-permute-start = (bf16[1,256,512]{2,1,0:T(8,128)(2,1)S(1)}, bf16[1,256,512]{2,1,0:T(8,128)(2,1)S(1)}, u32[]{:S(2)}, u32[]{:S(2)}) collective-permute-start(bf16[1,256,512]{2,1,0:T(8,128)(2,1)S(1)} %get-tuple-element.51), channel_id=1, source_target_pairs={{0,8},{8,16},{16,24},{24,32},{32,40},{40,48},{48,56},{1,9},{9,17},... | collective-permute-start | bytes 786440 | tf_op jit(solution)/shard_map/ppermute | solution.py:18
  7.1 9.1 %collective-permute-start.1 = (bf16[1,256,512]{2,1,0:T(8,128)(2,1)S(1)}, bf16[1,256,512]{2,1,0:T(8,128)(2,1)S(1)}, u32[]{:S(2)}, u32[]{:S(2)}) collective-permute-start(bf16[1,256,512]{2,1,0:T(8,128)(2,1)S(1)} %get-tuple-element.52), channel_id=1, source_target_pairs={{8,0},{16,8},{24,16},{32,24},{40,32},{48,40},{56,48},{9,1},{17,9},... | collective-permute-start | bytes 786440 | tf_op jit(solution)/shard_map/ppermute | solution.py:21
  9.6 6.7 %copy-start.2 = (bf16[1,4,256,256]{3,2,1,0:T(8,128)(2,1)S(1)}, bf16[1,4,256,256]{3,2,1,0:T(8,128)(2,1)}, u32[]{:S(2)}) copy-start(bf16[1,4,256,256]{3,2,1,0:T(8,128)(2,1)} %param.6) | copy-start | bytes 1572868
  9.6 13.7 %copy-start.7 = (bf16[1,4608,1024]{2,1,0:T(8,128)(2,1)S(1)}, bf16[1,4608,1024]{2,1,0:T(8,128)(2,1)}, u32[]{:S(2)}) copy-start(bf16[1,4608,1024]{2,1,0:T(8,128)(2,1)} %param.8) | copy-start | bytes 28311556
  16.3 13.6 %collective-permute-start.3 = (bf16[6,1,512]{2,1,0:T(2,128)(2,1)S(1)}, bf16[6,1,512]{2,1,0:T(2,128)(2,1)S(1)}, u32[]{:S(2)}, u32[]{:S(2)}) collective-permute-start(bf16[6,1,512]{2,1,0:T(2,128)(2,1)S(1)} %get-tuple-element.37), channel_id=1, source_target_pairs={{1,0},{2,1},{3,2},{4,3},{5,4},{6,5},{7,6},{9,8},{10,9},{11,10},{12... | collective-permute-start | bytes 18440 | tf_op jit(solution)/shard_map/ppermute | solution.py:21
  17.6 12.3 %collective-permute-start.2 = (bf16[6,1,512]{2,1,0:T(2,128)(2,1)S(1)}, bf16[6,1,512]{2,1,0:T(2,128)(2,1)S(1)}, u32[]{:S(2)}, u32[]{:S(2)}) collective-permute-start(bf16[6,1,512]{2,1,0:T(2,128)(2,1)S(1)} %get-tuple-element.38), channel_id=1, source_target_pairs={{0,1},{1,2},{2,3},{3,4},{4,5},{5,6},{6,7},{8,9},{9,10},{10,11},{11... | collective-permute-start | bytes 18440 | tf_op jit(solution)/shard_map/ppermute | solution.py:18
  45.0 3.3 %copy-start.3 = (f32[1024,1024]{1,0:T(8,128)S(1)}, f32[1024,1024]{1,0:T(8,128)}, u32[]{:S(2)}) copy-start(f32[1024,1024]{1,0:T(8,128)} %fusion.59) | copy-start | bytes 12582916
  48.3 10.2 %copy-start.6 = (f32[1,4,256,256]{3,2,1,0:T(8,128)S(1)}, f32[1,4,256,256]{3,2,1,0:T(8,128)}, u32[]{:S(2)}) copy-start(f32[1,4,256,256]{3,2,1,0:T(8,128)} %param.7) | copy-start | bytes 3145732
  58.5 7.0 %copy-start.4 = (bf16[2,4,256,256]{3,2,1,0:T(8,128)(2,1)S(1)}, bf16[2,4,256,256]{3,2,1,0:T(8,128)(2,1)}, u32[]{:S(2)}) copy-start(bf16[2,4,256,256]{3,2,1,0:T(8,128)(2,1)} %param.5) | copy-start | bytes 3145732
  60.6 4.9 %collective-permute-start.4 = (bf16[4,256,256]{2,1,0:T(8,128)(2,1)S(1)}, bf16[4,256,256]{2,1,0:T(8,128)(2,1)S(1)}, u32[]{:S(2)}, u32[]{:S(2)}) collective-permute-start(bf16[4,256,256]{2,1,0:T(8,128)(2,1)S(1)} %get-tuple-element.7), channel_id=1, source_target_pairs={{0,64},{1,65},{2,66},{3,67},{4,68},{5,69},{6,70},{7,71},{8,72},{9,... | collective-permute-start | bytes 1572872 | tf_op jit(solution)/shard_map/ppermute | solution.py:10
  65.6 8.9 %collective-permute-start.5 = (bf16[1,256,512]{2,1,0:T(8,128)(2,1)S(1)}, bf16[1,256,512]{2,1,0:T(8,128)(2,1)S(1)}, u32[]{:S(2)}, u32[]{:S(2)}) collective-permute-start(bf16[1,256,512]{2,1,0:T(8,128)(2,1)S(1)} %get-tuple-element.47), channel_id=1, source_target_pairs={{0,8},{8,16},{16,24},{24,32},{32,40},{40,48},{48,56},{1,9},{9,17},... | collective-permute-start | bytes 786440 | tf_op jit(solution)/shard_map/ppermute | solution.py:18
  68.9 9.3 %collective-permute-start.6 = (bf16[1,256,512]{2,1,0:T(8,128)(2,1)S(1)}, bf16[1,256,512]{2,1,0:T(8,128)(2,1)S(1)}, u32[]{:S(2)}, u32[]{:S(2)}) collective-permute-start(bf16[1,256,512]{2,1,0:T(8,128)(2,1)S(1)} %get-tuple-element.48), channel_id=1, source_target_pairs={{8,0},{16,8},{24,16},{32,24},{40,32},{48,40},{56,48},{9,1},{17,9},... | collective-permute-start | bytes 786440 | tf_op jit(solution)/shard_map/ppermute | solution.py:21
  78.3 16.6 %collective-permute-start.8 = (bf16[6,1,512]{2,1,0:T(2,128)(2,1)S(1)}, bf16[6,1,512]{2,1,0:T(2,128)(2,1)S(1)}, u32[]{:S(2)}, u32[]{:S(2)}) collective-permute-start(bf16[6,1,512]{2,1,0:T(2,128)(2,1)S(1)} %get-tuple-element.33), channel_id=1, source_target_pairs={{1,0},{2,1},{3,2},{4,3},{5,4},{6,5},{7,6},{9,8},{10,9},{11,10},{12... | collective-permute-start | bytes 18440 | tf_op jit(solution)/shard_map/ppermute | solution.py:21
  79.6 15.3 %collective-permute-start.7 = (bf16[6,1,512]{2,1,0:T(2,128)(2,1)S(1)}, bf16[6,1,512]{2,1,0:T(2,128)(2,1)S(1)}, u32[]{:S(2)}, u32[]{:S(2)}) collective-permute-start(bf16[6,1,512]{2,1,0:T(2,128)(2,1)S(1)} %get-tuple-element.34), channel_id=1, source_target_pairs={{0,1},{1,2},{2,3},{3,4},{4,5},{5,6},{6,7},{8,9},{9,10},{10,11},{11... | collective-permute-start | bytes 18440 | tf_op jit(solution)/shard_map/ppermute | solution.py:18
  86.3 5.3 %slice-start = ((s8[9437184]{0:T(1024)(128)(4,1)}), s8[4194304]{0:T(1024)(128)(4,1)S(1)}, s32[]{:S(2)}) async-start(s8[9437184]{0:T(1024)(128)(4,1)} %bitcast.155), calls=%async_computation | async-start | bytes 8388608
  86.3 5.3 %slice-start.1 = ((s8[9437184]{0:T(1024)(128)(4,1)}), s8[4194304]{0:T(1024)(128)(4,1)S(1)}, s32[]{:S(2)}) async-start(s8[9437184]{0:T(1024)(128)(4,1)} %bitcast.155), calls=%async_computation.1 | async-start | bytes 8388608
  88.9 2.6 %slice-start.2 = ((s8[9437184]{0:T(1024)(128)(4,1)}), s8[1048576]{0:T(1024)(128)(4,1)S(1)}, s32[]{:S(2)}) async-start(s8[9437184]{0:T(1024)(128)(4,1)} %bitcast.155), calls=%async_computation.2 | async-start | bytes 2097152
  123.2 7.0 %copy-start.5 = (bf16[2,4,256,256]{3,2,1,0:T(8,128)(2,1)S(1)}, bf16[2,4,256,256]{3,2,1,0:T(8,128)(2,1)}, u32[]{:S(2)}) copy-start(bf16[2,4,256,256]{3,2,1,0:T(8,128)(2,1)} %param.5) | copy-start | bytes 3145732
  125.7 4.5 %collective-permute-start.9 = (bf16[4,256,256]{2,1,0:T(8,128)(2,1)S(1)}, bf16[4,256,256]{2,1,0:T(8,128)(2,1)S(1)}, u32[]{:S(2)}, u32[]{:S(2)}) collective-permute-start(bf16[4,256,256]{2,1,0:T(8,128)(2,1)S(1)} %get-tuple-element.4), channel_id=1, source_target_pairs={{0,64},{1,65},{2,66},{3,67},{4,68},{5,69},{6,70},{7,71},{8,72},{9,... | collective-permute-start | bytes 1572872 | tf_op jit(solution)/shard_map/ppermute | solution.py:10
  131.1 9.8 %collective-permute-start.10 = (bf16[1,256,512]{2,1,0:T(8,128)(2,1)}, bf16[1,256,512]{2,1,0:T(8,128)(2,1)S(1)}, u32[]{:S(2)}, u32[]{:S(2)}) collective-permute-start(bf16[1,256,512]{2,1,0:T(8,128)(2,1)} %get-tuple-element.42), channel_id=1, source_target_pairs={{0,8},{8,16},{16,24},{24,32},{32,40},{40,48},{48,56},{1,9},{9,17},... | collective-permute-start | bytes 786440 | tf_op jit(solution)/shard_map/ppermute | solution.py:18
  135.1 9.7 %collective-permute-start.11 = (bf16[1,256,512]{2,1,0:T(8,128)(2,1)}, bf16[1,256,512]{2,1,0:T(8,128)(2,1)}, u32[]{:S(2)}, u32[]{:S(2)}) collective-permute-start(bf16[1,256,512]{2,1,0:T(8,128)(2,1)} %get-tuple-element.43), channel_id=1, source_target_pairs={{8,0},{16,8},{24,16},{32,24},{40,32},{48,40},{56,48},{9,1},{17,9},... | collective-permute-start | bytes 786440 | tf_op jit(solution)/shard_map/ppermute | solution.py:21
  145.5 18.0 %collective-permute-start.13 = (bf16[6,1,512]{2,1,0:T(2,128)(2,1)S(1)}, bf16[6,1,512]{2,1,0:T(2,128)(2,1)S(1)}, u32[]{:S(2)}, u32[]{:S(2)}) collective-permute-start(bf16[6,1,512]{2,1,0:T(2,128)(2,1)S(1)} %get-tuple-element.29), channel_id=1, source_target_pairs={{1,0},{2,1},{3,2},{4,3},{5,4},{6,5},{7,6},{9,8},{10,9},{11,10},{12... | collective-permute-start | bytes 18440 | tf_op jit(solution)/shard_map/ppermute | solution.py:21
  146.8 16.7 %collective-permute-start.12 = (bf16[6,1,512]{2,1,0:T(2,128)(2,1)S(1)}, bf16[6,1,512]{2,1,0:T(2,128)(2,1)S(1)}, u32[]{:S(2)}, u32[]{:S(2)}) collective-permute-start(bf16[6,1,512]{2,1,0:T(2,128)(2,1)S(1)} %get-tuple-element.30), channel_id=1, source_target_pairs={{0,1},{1,2},{2,3},{3,4},{4,5},{5,6},{6,7},{8,9},{9,10},{10,11},{11... | collective-permute-start | bytes 18440 | tf_op jit(solution)/shard_map/ppermute | solution.py:18
  154.9 5.3 %slice-start.3 = ((s8[9437184]{0:T(1024)(128)(4,1)}), s8[4194304]{0:T(1024)(128)(4,1)S(1)}, s32[]{:S(2)}) async-start(s8[9437184]{0:T(1024)(128)(4,1)} %bitcast.157), calls=%async_computation.3 | async-start | bytes 8388608
  154.9 5.3 %slice-start.4 = ((s8[9437184]{0:T(1024)(128)(4,1)}), s8[4194304]{0:T(1024)(128)(4,1)S(1)}, s32[]{:S(2)}) async-start(s8[9437184]{0:T(1024)(128)(4,1)} %bitcast.157), calls=%async_computation.4 | async-start | bytes 8388608
  157.6 2.6 %slice-start.5 = ((s8[9437184]{0:T(1024)(128)(4,1)}), s8[1048576]{0:T(1024)(128)(4,1)S(1)}, s32[]{:S(2)}) async-start(s8[9437184]{0:T(1024)(128)(4,1)} %bitcast.157), calls=%async_computation.5 | async-start | bytes 2097152
  195.4 2.9 %copy-start.1 = (f32[2,1024]{1,0:T(2,128)S(1)}, f32[2,1024]{1,0:T(2,128)}, u32[]{:S(2)}) copy-start(f32[2,1024]{1,0:T(2,128)} %param.9) | copy-start | bytes 24580
where the time goes:
time: 201 us; the launch traced here: 198 us
  matrix products  107 us (53%)
  starting transfers between devices  40.9 us (20%)
  waiting for transfers between devices  27 us (13%)
  other arithmetic  19.3 us (10%)
  local copies, waits for them, and re-layouts  3.24 us (2%)
    dot_general x27, matrix products, tile_gates(): jnp.dot(window, kernel[tap * width:(tap + 1) * width], preferred_element_...  107 us
    ppermute x6, starting transfers between devices, extended(): lax.ppermute(lax.slice_in_dim(block, block.shape[dim] - width, None, axis...  30.4 us
    ppermute x6, waiting for transfers between devices, extended(): lax.ppermute(lax.slice_in_dim(block, 0, width, axis=dim), axis, backward)  11.5 us
    ppermute x6, waiting for transfers between devices, extended(): lax.ppermute(lax.slice_in_dim(block, block.shape[dim] - width, None, axis...  8.6 us
    ppermute x6, starting transfers between devices, extended(): lax.ppermute(lax.slice_in_dim(block, 0, width, axis=dim), axis, backward)  7.93 us
    concatenate x9, other arithmetic, extended(): block = jnp.concatenate([low, block, high], axis=dim)  7.73 us
    ppermute x2, waiting for transfers between devices, passed_along(): lax.ppermute(value, axis, [(source, source + steps) for source in range(l...  6.86 us
    select_n x2, other arithmetic, per_device(): hidden = jnp.where(active, new_hidden, hidden)  4.54 us
  transfers between devices with their start and end apart: 14, of which 7 were waited for; matrix products, arithmetic and copies ran while one was open for 15% of the time, Pallas kernels for 0%

commit v1 on v0

v1 whole, which is shorter than its diff:
```python
import jax
import jax.numpy as jnp
from jax import lax
from jax.experimental import pallas as pl
from jax.experimental.pallas import tpu as pltpu
from jax.sharding import PartitionSpec as P

f32 = jnp.float32
bf16 = jnp.bfloat16
ROWS, COLS, CH, GATES = 4, 256, 256, 1024
PAD = 8
EXT = COLS + 2 * PAD
LO, HI = 16, EXT - 16
NB = 512

ANYV = pl.BlockSpec(memory_space=pltpu.VMEM)
SM = pl.BlockSpec(memory_space=pltpu.SMEM)


def vm(shape, dtype):
    return pltpu.VMEM(shape, dtype)


def call(body, outs, args, aliases=None, scratch=(), flops=0, limit=14):
    specs = [SM] + [ANYV] * (len(args) - 1)
    return pl.pallas_call(
        body,
        in_specs=specs,
        out_specs=[ANYV] * len(outs),
        out_shape=list(outs),
        scratch_shapes=list(scratch),
        input_output_aliases=aliases or {},
        compiler_params=pltpu.CompilerParams(vmem_limit_bytes=limit << 20),
        cost_estimate=pl.CostEstimate(flops=flops, bytes_accessed=1 << 20, transcendentals=0),
    )(*args)


def shifted(x, store):
    n = x.shape[0]
    store(0, pltpu.roll(x, 1, 0).astype(bf16))
    store(1, x.astype(bf16))
    store(2, pltpu.roll(x, n - 1, 0).astype(bf16))


def build(stack, r, mid, left=None, right=None):
    mid = mid.astype(f32)
    if mid.shape[0] == COLS:
        zero = jnp.zeros((PAD, CH), f32)
        mid = jnp.concatenate([zero, mid, zero], axis=0)

    def store(dx, v):
        stack[dx, r] = v

    shifted(mid, store)


def columns(body):
    def step(n, carry):
        body(pl.ds(pl.multiple_of(n * NB, NB), NB))
        return carry

    lax.fori_loop(0, GATES // NB, step, 0)


def taps(w, c, lhs, off, tap, total):
    d = jnp.dot(lhs, w[pl.ds(tap * 512 + off, 256), c], preferred_element_type=f32)
    return d if total is None else total + d


def inner(acc, w, parts, c, lo, hi, add):
    for r in range(ROWS):
        total = acc[r, lo:hi, c] if add else None
        for dy in range(3):
            q = r + dy - 1
            if 0 <= q < ROWS:
                for dx in range(3):
                    for stack, off in parts:
                        total = taps(w, c, stack[dx, q, lo:hi, :], off, 3 * dy + dx, total)
        acc[r, lo:hi, c] = total


def outer(acc, w, parts, c, lo, hi):
    for r, q, dy in ((0, 0, 0), (ROWS - 1, 1, 2)):
        total = acc[r, lo:hi, c]
        for dx in range(3):
            for stack, off in parts:
                total = taps(w, c, stack[dx, q, lo:hi, :], off, 3 * dy + dx, total)
        acc[r, lo:hi, c] = total


def sigmoid(x):
    return 0.5 * jnp.tanh(0.5 * x) + 0.5


def epilogue(sc, acc, bias, cell_at, put):
    core, gx = sc[0], sc[1]
    b = bias[pl.ds(core, 1), :]

    def step(k, carry):
        at = pl.ds(pl.multiple_of(k * 16, 16), 16)
        col = lax.broadcasted_iota(jnp.int32, (16, CH), 0) + k * 16
        inside = jnp.logical_and(
            jnp.logical_or(gx > 0, col >= PAD), jnp.logical_or(gx < sc[2] - 1, col < PAD + COLS)
        )
        for r in range(ROWS):
            g = [acc[r, at, i * CH : (i + 1) * CH] + b[:, i * CH : (i + 1) * CH] for i in range(4)]
            cell = sigmoid(g[1]) * cell_at(r, at) + sigmoid(g[0]) * jnp.tanh(g[3])
            hid = sigmoid(g[2]) * jnp.tanh(cell)
            put(r, at, cell, jnp.where(inside, hid, 0.0))
        return carry

    lax.fori_loop(0, EXT // 16, step, 0)


def k_first(sc, fr, hid, w, acc_a, acc_b, s_f, s_h):
    core = sc[0]
    for r in range(ROWS):
        build(s_h, r, hid[0, r])

    @pl.when(core == 0)
    def _():
        for r in range(ROWS):
            build(s_f, r, fr[0, r])
        columns(lambda c: inner(acc_a, w, ((s_f, 0), (s_h, 256)), c, LO, HI, False))

    @pl.when(core == 1)
    def _():
        columns(lambda c: inner(acc_b, w, ((s_h, 256),), c, LO, HI, False))


def k_second(sc, fr, w, yt, yb, acc_a, acc_b, out_a, out_b, s_f, halo):
    core = sc[0]
    for i in range(3):
        build(halo.at[i], 0, yt[i])
        build(halo.at[i], 1, yb[i])

    @pl.when(core == 0)
    def _():
        for r in range(ROWS):
            build(s_f, r, fr[1, r])

        def body(c):
            outer(acc_a, w, ((halo.at[0], 0), (halo.at[2], 256)), c, LO, HI)
            inner(acc_b, w, ((s_f, 0),), c, LO, HI, False)
            outer(acc_b, w, ((halo.at[1], 0),), c, LO, HI)

        columns(body)

    @pl.when(core == 1)
    def _():
        columns(lambda c: outer(acc_b, w, ((halo.at[2], 256),), c, LO, HI))


def strip(s, i, rows, left, right):
    for r in range(ROWS + 2):
        row = rows(r)
        a = jnp.concatenate([left[i, r].astype(f32), row[0:16].astype(f32)], axis=0)
        b = jnp.concatenate([row[COLS - 16 : COLS].astype(f32), right[i, r].astype(f32)], axis=0)

        def store_a(dx, v):
            s[dx, r, 0:16, :] = v[0:16]

        def store_b(dx, v):
            s[dx, r, 16:32, :] = v[8:24]

        n = 24
        for dx, k in ((0, 1), (1, 0), (2, n - 1)):
            av = pltpu.roll(a, k, 0) if k else a
            bv = pltpu.roll(b, k, 0) if k else b
            s[dx, r, 0:16, :] = av[0:16].astype(bf16)
            s[dx, r, 16:32, :] = bv[8:24].astype(bf16)


def sides(acc, w, parts, c):
    total = None
    for dy in range(3):
        for dx in range(3):
            for s, off in parts:
                lhs = s[dx, dy : dy + ROWS].reshape(ROWS * 32, CH)
                total = taps(w, c, lhs, off, 3 * dy + dx, total)
    for r in range(ROWS):
        acc[r, 0:LO, c] = total[r * 32 : r * 32 + 16]
        acc[r, HI:EXT, c] = total[r * 32 + 16 : r * 32 + 32]


def k_sides(sc, fr, hid, cell, w, bias, yt, yb, left, right, cl, cr, acc_a, acc_b, out_a, out_b, h, cx, s):
    core = sc[0]

    def rows_of(i, tile):
        def rows(r):
            if r == 0:
                return yt[i]
            if r == ROWS + 1:
                return yb[i]
            return tile[r - 1]

        return rows

    strip(s.at[2], 2, rows_of(2, hid.at[0]), left, right)
    for r in range(ROWS):
        cx[r, 0:PAD] = cl[0, r].astype(f32) + cl[1, r].astype(f32)
        cx[r, PAD : PAD + COLS] = cell[0, r]
        cx[r, PAD + COLS : EXT] = cr[0, r].astype(f32) + cr[1, r].astype(f32)

    @pl.when(core == 0)
    def _():
        strip(s.at[0], 0, rows_of(0, fr.at[0]), left, right)
        strip(s.at[1], 1, rows_of(1, fr.at[1]), left, right)

        def body(c):
            sides(acc_a, w, ((s.at[0], 0), (s.at[2], 256)), c)
            sides(acc_b, w, ((s.at[1], 0),), c)

        columns(body)

        def put(r, at, new, hd):
            cx[r, at] = new
            h[r, at] = hd.astype(bf16)

        epilogue(sc, acc_a, bias, lambda r, at: cx[r, at], put)

    @pl.when(core == 1)
    def _():
        h[...] = jnp.zeros((ROWS, EXT, CH), bf16)
        columns(lambda c: sides(acc_b, w, ((s.at[2], 256),), c))


def k_third(sc, h, recv, w, acc_b, out_b, s):
    core = sc[0]

    @pl.when(core == 0)
    def _():
        for r in range(ROWS):
            build(s, r, h[r])

    @pl.when(core == 1)
    def _():
        for r in range(ROWS):
            build(s, r, recv[r])

    off = pl.multiple_of((1 - core) * 256, 256)
    columns(lambda c: inner(acc_b, w, ((s, off),), c, 0, EXT, True))


def k_fourth(sc, top, bot, w, bias, cx, acc_b, out_b, h, cx2, s):
    core = sc[0]
    build(s, 0, top[...])
    build(s, 1, bot[...])
    off = pl.multiple_of((1 - core) * 256, 256)
    columns(lambda c: outer(acc_b, w, ((s, off),), c, 0, EXT))

    def put(r, at, new, hd):
        cx2[r, at] = new
        h[r, at] = hd.astype(bf16)

    epilogue(sc, acc_b, bias, lambda r, at: cx[r, at], put)


def k_fifth(sc, h, w, acc, s):
    @pl.when(sc[0] == 1)
    def _():
        for r in range(ROWS):
            build(s, r, h[r])
        columns(lambda c: inner(acc, w, ((s, 256),), c, 0, EXT, False))


def k_sixth(sc, top, bot, w, acc, out, s):
    @pl.when(sc[0] == 1)
    def _():
        build(s, 0, top[...])
        build(s, 1, bot[...])
        columns(lambda c: outer(acc, w, ((s, 256),), c, 0, EXT))


def k_last(sc, recv, h, cx, w, bias, acc, out, ho, co, s, s2):
    core = sc[0]

    @pl.when(core == 0)
    def _():
        for r in range(ROWS):
            ho[0, r] = h[r].astype(f32)[PAD : PAD + COLS].astype(bf16)
            co[0, r] = cx[r, PAD : PAD + COLS]

    @pl.when(core == 1)
    def _():
        for r in range(ROWS):
            build(s, r, recv[r + 1])
        build(s2, 0, recv[0])
        build(s2, 1, recv[ROWS + 1])

        def body(c):
            inner(acc, w, ((s, 0),), c, 0, EXT, True)
            outer(acc, w, ((s2, 0),), c, 0, EXT)

        columns(body)
        b = bias[pl.ds(core, 1), :]

        def step(k, carry):
            at = pl.ds(pl.multiple_of(k * 16, 16), 16)
            src = pl.ds(pl.multiple_of(k * 16 + PAD, 8), 16)
            for r in range(ROWS):
                g = [acc[r, src, i * CH : (i + 1) * CH] + b[:, i * CH : (i + 1) * CH] for i in range(4)]
                new = sigmoid(g[1]) * cx[r, src] + sigmoid(g[0]) * jnp.tanh(g[3])
                co[0, r, at] = new
                ho[0, r, at] = (sigmoid(g[2]) * jnp.tanh(new)).astype(bf16)
            return carry

        lax.fori_loop(0, COLS // 16, step, 0)


UNIT = 2 * ROWS * COLS * 4608 * 1024
ACC = (ROWS, EXT, GATES)
TILE = (ROWS, EXT, CH)
STACK = (3, ROWS, EXT, CH)
PAIR = (3, 2, EXT, CH)


def along(axis, count):
    up = [(i, i + 1) for i in range(count - 1)]
    return up, [(b, a) for a, b in up]


def per_device(frames, hidden_init, cell_init, conv_weight, conv_bias):
    core = lax.axis_index("layer")
    ny, nx = lax.axis_size("gy"), lax.axis_size("gx")
    sc = jnp.stack([core, lax.axis_index("gx"), jnp.int32(nx)]).astype(jnp.int32)
    w = pltpu.with_memory_space_constraint(conv_weight[0], pltpu.VMEM)
    down, up = along("gy", ny)
    right, left = along("gx", nx)
    swap = [(0, 1), (1, 0)]

    def edge_rows(r):
        return jnp.concatenate([frames[:, r], hidden_init[:, r]], axis=0)

    yt = lax.ppermute(edge_rows(ROWS - 1), "gy", down)
    yb = lax.ppermute(edge_rows(0), "gy", up)

    acc_a, acc_b = call(
        k_first,
        [vm(ACC, f32), vm(ACC, f32)],
        [sc, frames, hidden_init, w],
        scratch=[pltpu.VMEM(STACK, bf16)] * 2,
        flops=int(UNIT * 0.75),
    )

    hi = lax.reduce_precision(cell_init[0], 8, 7)
    rest = cell_init[0] - hi

    def edge_cols(a, b):
        six = jnp.concatenate(
            [
                yt[:, None, a:b],
                jnp.concatenate([frames[:, :, a:b], hidden_init[:, :, a:b]], axis=0),
                yb[:, None, a:b],
            ],
            axis=1,
        ).reshape(18, b - a, CH)
        return jnp.concatenate([six, hi[:, a:b].astype(bf16), rest[:, a:b].astype(bf16)], axis=0)

    from_left = lax.ppermute(edge_cols(COLS - PAD, COLS), "gx", right)
    from_right = lax.ppermute(edge_cols(0, PAD), "gx", left)

    acc_a, acc_b = call(
        k_second,
        [vm(ACC, f32), vm(ACC, f32)],
        [sc, frames, w, yt, yb, acc_a, acc_b],
        aliases={5: 0, 6: 1},
        scratch=[pltpu.VMEM(STACK, bf16), pltpu.VMEM((3,) + PAIR, bf16)],
        flops=int(UNIT * 0.55),
    )

    def six_of(m):
        return m[:18].reshape(3, 6, PAD, CH), m[18:].reshape(2, ROWS, PAD, CH)

    l6, cl = six_of(from_left)
    r6, cr = six_of(from_right)
    acc_a, acc_b, h, cx = call(
        k_sides,
        [vm(ACC, f32), vm(ACC, f32), vm(TILE, bf16), vm(TILE, f32)],
        [sc, frames, hidden_init, cell_init, w, conv_bias, yt, yb, l6, r6, cl, cr, acc_a, acc_b],
        aliases={12: 0, 13: 1},
        scratch=[pltpu.VMEM((3, 3, 6, 32, CH), bf16)],
        flops=int(UNIT * 0.25),
        limit=20,
    )

    recv = lax.ppermute(h, "layer", swap)
    src = jnp.where(core == 0, h, recv)
    top = lax.ppermute(src[ROWS - 1], "gy", down)
    bot = lax.ppermute(src[0], "gy", up)
    (acc_b,) = call(
        k_third,
        [vm(ACC, f32)],
        [sc, h, recv, w, acc_b],
        aliases={4: 0},
        scratch=[pltpu.VMEM(STACK, bf16)],
        flops=int(UNIT * 0.42),
    )
    acc_b, h2, cx2 = call(
        k_fourth,
        [vm(ACC, f32), vm(TILE, bf16), vm(TILE, f32)],
        [sc, top, bot, w, conv_bias, cx, acc_b],
        aliases={6: 0},
        scratch=[pltpu.VMEM(PAIR, bf16)],
        flops=int(UNIT * 0.16),
    )

    top2 = lax.ppermute(h2[ROWS - 1], "gy", down)
    bot2 = lax.ppermute(h2[0], "gy", up)
    (acc,) = call(
        k_fifth,
        [vm(ACC, f32)],
        [sc, h2, w],
        scratch=[pltpu.VMEM(STACK, bf16)],
        flops=int(UNIT * 0.42),
    )
    (acc,) = call(
        k_sixth,
        [vm(ACC, f32)],
        [sc, top2, bot2, w, acc],
        aliases={4: 0},
        scratch=[pltpu.VMEM(PAIR, bf16)],
        flops=int(UNIT * 0.08),
    )
    six = jnp.concatenate([top2[None], h2, bot2[None]], axis=0)
    six, acc = lax.optimization_barrier((six, acc))
    recv2 = lax.ppermute(six, "layer", swap)
    acc, ho, co = call(
        k_last,
        [
            vm(ACC, f32),
            jax.ShapeDtypeStruct((1, ROWS, COLS, CH), bf16),
            jax.ShapeDtypeStruct((1, ROWS, COLS, CH), f32),
        ],
        [sc, recv2, h2, cx2, w, conv_bias, acc],
        aliases={6: 0},
        scratch=[pltpu.VMEM(STACK, bf16), pltpu.VMEM(PAIR, bf16)],
        flops=int(UNIT * 0.5),
    )
    return ho, co


def solution(mesh):
    placed = (
        P(None, "gy", "gx", None),
        P("layer", "gy", "gx", None),
        P("layer", "gy", "gx", None),
        P("layer", None, None),
        P(),
    )
    return jax.shard_map(
        per_device,
        mesh=mesh,
        in_specs=placed,
        out_specs=(P("layer", "gy", "gx", None), P("layer", "gy", "gx", None)),
        check_vma=False,
    )
```

time: 201 us -> 100 us (0.50)
  the two profiles are of different devices: /device:TPU:1 before, /device:TPU:15 now
where the time goes in v1:
time: 100 us; the launch traced here: 99.9 us
  starting transfers between devices  40.8 us (41%)
  Pallas kernels  33.6 us (34%)
  local copies, waits for them, and re-layouts  15.8 us (16%)
  waiting for transfers between devices  5.3 us (5%)
  other arithmetic  3.24 us (3%)
  between operations  1.12 us (1%)
    pallas_call x8, Pallas kernels, call(): pl.pallas_call(body, in_specs=specs, out_specs=[ANYV] * len(outs), out_sh...  33.6 us
    unnamed x34, local copies, waits for them, and re-layouts  12.8 us
    ppermute x1, starting transfers between devices, per_device(): recv = lax.ppermute(h, 'layer', swap)  12.6 us
    ppermute x1, starting transfers between devices, per_device(): bot2 = lax.ppermute(h2[0], 'gy', up)  5.74 us
    ppermute x1, starting transfers between devices, per_device(): from_left = lax.ppermute(edge_cols(COLS - PAD, COLS), 'gx', right)  4.22 us
    ppermute x1, starting transfers between devices, per_device(): yb = lax.ppermute(edge_rows(0), 'gy', up)  3.91 us
    ppermute x1, starting transfers between devices, per_device(): yt = lax.ppermute(edge_rows(ROWS - 1), 'gy', down)  3.53 us
    ppermute x1, starting transfers between devices, per_device(): from_right = lax.ppermute(edge_cols(0, PAD), 'gx', left)  3.46 us
  transfers between devices with their start and end apart: 10, of which 3 were waited for; matrix products, arithmetic and copies ran while one was open for 3% of the time, Pallas kernels for 18%

profile of v1, /device:TPU:15, one launch (start us, length us, event | category | flops | bytes accessed | tf_op | source)
XLA Modules:
  0.0 99.9 jit_solution(4889444300346147543)
XLA Ops:
  0.7 1.1 %slice_bitcast_fusion.6 = (bf16[1,256,256]{2,1,0:T(8,128)(2,1)S(1)}, bf16[1,256,256]{2,1,0:T(8,128)(2,1)S(1)}) fusion(bf16[1,4,256,256]{3,2,1,0:T(8,128)(2,1)} %hid.3), kind=kLoop, calls=%fused_computation.13 | loop fusion | bytes 524288 | tf_op jit(solution)/shard_map/squeeze | solution.py:333
  1.8 1.1 %slice_bitcast_fusion = (bf16[2,256,256]{2,1,0:T(8,128)(2,1)S(1)}, bf16[2,256,256]{2,1,0:T(8,128)(2,1)S(1)}) fusion(bf16[2,4,256,256]{3,2,1,0:T(8,128)(2,1)} %fr.5), kind=kLoop, calls=%fused_computation.7 | loop fusion | bytes 1048576 | tf_op jit(solution)/shard_map/squeeze | solution.py:333
  2.8 0.8 pad_maximum_fusion.1
  3.6 3.5 %collective-permute-start = (bf16[3,256,256]{2,1,0:T(8,128)(2,1)}, bf16[3,256,256]{2,1,0:T(8,128)(2,1)S(1)}, u32[]{:S(2)}, u32[]{:S(2)}) collective-permute-start(bf16[3,256,256]{2,1,0:T(8,128)(2,1)} %pad_maximum_fusion.1), channel_id=1, source_target_pairs={{0,8},{8,16},{16,24},{24,32},{32,40},{40,48},{48,56},{1,9},{9,17},... | collective-permute-start | bytes 1179656 | tf_op jit(solution)/shard_map/ppermute | solution.py:335
  7.2 0.8 pad_maximum_fusion.2
  8.0 3.9 %collective-permute-start.1 = (bf16[3,256,256]{2,1,0:T(8,128)(2,1)}, bf16[3,256,256]{2,1,0:T(8,128)(2,1)S(1)}, u32[]{:S(2)}, u32[]{:S(2)}) collective-permute-start(bf16[3,256,256]{2,1,0:T(8,128)(2,1)} %pad_maximum_fusion.2), channel_id=1, source_target_pairs={{8,0},{16,8},{24,16},{32,24},{40,32},{48,40},{56,48},{9,1},{17,9},... | collective-permute-start | bytes 1179656 | tf_op jit(solution)/shard_map/ppermute | solution.py:336
  11.9 0.8 fusion.1
  12.7 1.4 %reduce-precision_convert_fusion = (bf16[4,256,256]{2,1,0:T(8,128)(2,1)S(1)}, bf16[4,256,256]{2,1,0:T(8,128)(2,1)S(1)}) fusion(f32[1,4,256,256]{3,2,1,0:T(8,128)} %cell.1), kind=kLoop, calls=%fused_computation.1 | loop fusion | flops 1048576 | bytes 2097152 | tf_op jit(solution)/shard_map/convert.3
  14.1 3.7 %copy-done = bf16[1,4608,1024]{2,1,0:T(8,128)(2,1)S(1)} copy-done((bf16[1,4608,1024]{2,1,0:T(8,128)(2,1)S(1)}, bf16[1,4608,1024]{2,1,0:T(8,128)(2,1)}, u32[]{:S(2)}) %copy-start) | copy-done | bytes 9437208
  17.8 5.0 %shard_map.68 = (f32[4,272,1024]{2,1,0:T(8,128)S(1)}, f32[4,272,1024]{2,1,0:T(8,128)S(1)}) custom-call(s32[3]{0:T(128)S(1)} %pad_add_fusion.sc, bf16[2,4,256,256]{3,2,1,0:T(8,128)(2,1)S(1)} %copy-done.4, bf16[1,4,256,256]{3,2,1,0:T(8,128)(2,1)S(1)} %copy-done.6, bf16[4608,1024]{1,0:T(8,128)(2,1)S(1)} %bitcast.50), custom_call_target="tpu_custom_call" | custom-call | flops 7247757312 | bytes 1048576 | tf_op jit(solution)/shard_map/pallas_call | solution.py:26
  23.0 4.2 %collective-permute-start.2 = (bf16[26,8,256]{2,1,0:T(8,128)(2,1)S(1)}, bf16[26,8,256]{2,1,0:T(8,128)(2,1)S(1)}, u32[]{:S(2)}, u32[]{:S(2)}) collective-permute-start(bf16[26,8,256]{2,1,0:T(8,128)(2,1)S(1)} %pad_maximum_fusion.3), channel_id=1, source_target_pairs={{0,1},{1,2},{2,3},{3,4},{4,5},{5,6},{6,7},{8,9},{9,10},{10,11},{11... | collective-permute-start | bytes 319496 | tf_op jit(solution)/shard_map/ppermute | solution.py:360
  27.2 3.5 %collective-permute-start.3 = (bf16[26,8,256]{2,1,0:T(8,128)(2,1)S(1)}, bf16[26,8,256]{2,1,0:T(8,128)(2,1)S(1)}, u32[]{:S(2)}, u32[]{:S(2)}) collective-permute-start(bf16[26,8,256]{2,1,0:T(8,128)(2,1)S(1)} %pad_maximum_fusion.4), channel_id=1, source_target_pairs={{1,0},{2,1},{3,2},{4,3},{5,4},{6,5},{7,6},{9,8},{10,9},{11,10},{12... | collective-permute-start | bytes 319496 | tf_op jit(solution)/shard_map/ppermute | solution.py:361
  30.8 2.0 %shard_map.69 = (f32[4,272,1024]{2,1,0:T(8,128)S(1)}, f32[4,272,1024]{2,1,0:T(8,128)S(1)}) custom-call(s32[3]{0:T(128)S(1)} %pad_add_fusion.sc, bf16[2,4,256,256]{3,2,1,0:T(8,128)(2,1)S(1)} %copy-done.4, bf16[4608,1024]{1,0:T(8,128)(2,1)S(1)} %bitcast.53, ...), custom_call_target="tpu_custom_call", output_to_operand_aliasing={{0}: (5, {}), {1}: (6, {})} | custom-call | flops 5315021824 | bytes 1048576 | tf_op jit(solution)/shard_map/pallas_call | solution.py:26
  32.8 1.4 %collective-permute-done.3 = bf16[26,8,256]{2,1,0:T(8,128)(2,1)S(1)} collective-permute-done((bf16[26,8,256]{2,1,0:T(8,128)(2,1)S(1)}, bf16[26,8,256]{2,1,0:T(8,128)(2,1)S(1)}, u32[]{:S(2)}, u32[]{:S(2)}) %collective-permute-start.3) | collective-permute-done | bytes 106528 | tf_op jit(solution)/shard_map/ppermute | solution.py:361
  34.2 1.7 %shard_map.70 = (f32[4,272,1024]{2,1,0:T(8,128)S(1)}, f32[4,272,1024]{2,1,0:T(8,128)S(1)}, bf16[4,272,256]{2,1,0:T(8,128)(2,1)S(1)}, f32[4,272,256]{2,1,0:T(8,128)S(1)}) custom-call(s32[3]{0:T(128)S(1)} %pad_add_fusion.sc, bf16[2,4,256,256]{3,2,1,0:T(8,128)(2,1)S(1)} %copy-done.4, ...), custom_call_target="tpu_custom_call", output_to_operand_aliasing={{0}: (12, {}), {1}: (13, {})} | custom-call | flops 2415919104 | bytes 1048576 | tf_op jit(solution)/shard_map/pallas_call | solution.py:26
  35.9 2.1 %copy-done.2 = f32[4,272,1024]{2,1,0:T(8,128)} copy-done((f32[4,272,1024]{2,1,0:T(8,128)}, f32[4,272,1024]{2,1,0:T(8,128)S(1)}, u32[]{:S(2)}) %copy-start.2) | copy-done | bytes 4456472
  37.9 1.0 %copy-done.8 = f32[4,272,256]{2,1,0:T(8,128)} copy-done((f32[4,272,256]{2,1,0:T(8,128)}, f32[4,272,256]{2,1,0:T(8,128)S(1)}, u32[]{:S(2)}) %copy-start.8) | copy-done | bytes 1114136
  39.0 12.6 %collective-permute-start.4 = (bf16[4,272,256]{2,1,0:T(8,128)(2,1)S(1)}, bf16[4,272,256]{2,1,0:T(8,128)(2,1)S(1)}, u32[]{:S(2)}, u32[]{:S(2)}) collective-permute-start(bf16[4,272,256]{2,1,0:T(8,128)(2,1)S(1)} %get-tuple-element.19.h), channel_id=1, source_target_pairs={{0,64},{64,0},{1,65},{65,1},{2,66},{66,2},{3,67},{67,3},{4,68},{68... | collective-permute-start | bytes 1671176 | tf_op jit(solution)/shard_map/ppermute | solution.py:387
  51.6 1.6 %collective-permute-done.4.recv = bf16[4,272,256]{2,1,0:T(8,128)(2,1)S(1)} collective-permute-done((bf16[4,272,256]{2,1,0:T(8,128)(2,1)S(1)}, bf16[4,272,256]{2,1,0:T(8,128)(2,1)S(1)}, u32[]{:S(2)}, u32[]{:S(2)}) %collective-permute-start.4) | collective-permute-done | bytes 557088 | tf_op jit(solution)/shard_map/ppermute | solution.py:387
  53.2 3.4 %collective-permute-start.6 = (bf16[272,256]{1,0:T(8,128)(2,1)S(1)}, bf16[272,256]{1,0:T(8,128)(2,1)S(1)}, u32[]{:S(2)}, u32[]{:S(2)}) collective-permute-start(bf16[272,256]{1,0:T(8,128)(2,1)S(1)} %get-tuple-element.36), channel_id=1, source_target_pairs={{8,0},{16,8},{24,16},{32,24},{40,32},{48,40},{56,48},{9,1},{17,9},... | collective-permute-start | bytes 417800 | tf_op jit(solution)/shard_map/ppermute | solution.py:390
  56.7 1.9 %collective-permute-start.5 = (bf16[272,256]{1,0:T(8,128)(2,1)S(1)}, bf16[272,256]{1,0:T(8,128)(2,1)S(1)}, u32[]{:S(2)}, u32[]{:S(2)}) collective-permute-start(bf16[272,256]{1,0:T(8,128)(2,1)S(1)} %get-tuple-element.37), channel_id=1, source_target_pairs={{0,8},{8,16},{16,24},{24,32},{32,40},{40,48},{48,56},{1,9},{9,17},... | collective-permute-start | bytes 417800 | tf_op jit(solution)/shard_map/ppermute | solution.py:389
  58.6 3.7 %copy-done.1 = bf16[1,4608,1024]{2,1,0:T(8,128)(2,1)S(1)} copy-done((bf16[1,4608,1024]{2,1,0:T(8,128)(2,1)S(1)}, bf16[1,4608,1024]{2,1,0:T(8,128)(2,1)}, u32[]{:S(2)}) %copy-start.1) | copy-done | bytes 9437208
  62.3 2.3 %copy-done.3 = f32[4,272,1024]{2,1,0:T(8,128)S(1)} copy-done((f32[4,272,1024]{2,1,0:T(8,128)S(1)}, f32[4,272,1024]{2,1,0:T(8,128)}, u32[]{:S(2)}) %copy-start.3) | copy-done | bytes 4456472
  64.6 5.8 %shard_map.71.acc_b = f32[4,272,1024]{2,1,0:T(8,128)S(1)} custom-call(s32[3]{0:T(128)S(1)} %pad_add_fusion.sc, bf16[4,272,256]{2,1,0:T(8,128)(2,1)S(1)} %get-tuple-element.19.h, bf16[4,272,256]{2,1,0:T(8,128)(2,1)S(1)} %collective-permute-done.4.recv, bf16[4608,1024]{1,0:T(8,128)(2,1)S(1)} %bitcast.55, ...), custom_call_target="tpu_custom_call", output_to_operand_aliasing={{}: (4, {})} | custom-call | flops 4058744064 | bytes 1048576 | tf_op jit(solution)/shard_map/pallas_call | solution.py:26
  70.4 3.0 %shard_map.72 = (f32[4,272,1024]{2,1,0:T(8,128)S(1)}, bf16[4,272,256]{2,1,0:T(8,128)(2,1)S(1)}, f32[4,272,256]{2,1,0:T(8,128)S(1)}) custom-call(s32[3]{0:T(128)S(1)} %pad_add_fusion.sc, bf16[272,256]{1,0:T(8,128)(2,1)S(1)} %collective-permute-done.5.top, bf16[272,256]{1,0:T(8,128)(2,1)S(1)} %collective-permute-done.6.bot, ...), custom_call_target="tpu_custom_call", output_to_operand_aliasing={{0}: (6, {})} | custom-call | flops 1546188288 | bytes 1048576 | tf_op jit(solution)/shard_map/pallas_call | solution.py:26
  73.4 1.9 %collective-permute-start.7 = (bf16[272,256]{1,0:T(8,128)(2,1)S(1)}, bf16[272,256]{1,0:T(8,128)(2,1)S(1)}, u32[]{:S(2)}, u32[]{:S(2)}) collective-permute-start(bf16[272,256]{1,0:T(8,128)(2,1)S(1)} %get-tuple-element.34), channel_id=1, source_target_pairs={{0,8},{8,16},{16,24},{24,32},{32,40},{40,48},{48,56},{1,9},{9,17},... | collective-permute-start | bytes 417800 | tf_op jit(solution)/shard_map/ppermute | solution.py:408
  75.4 5.7 %collective-permute-start.8 = (bf16[272,256]{1,0:T(8,128)(2,1)S(1)}, bf16[272,256]{1,0:T(8,128)(2,1)S(1)}, u32[]{:S(2)}, u32[]{:S(2)}) collective-permute-start(bf16[272,256]{1,0:T(8,128)(2,1)S(1)} %get-tuple-element.35), channel_id=1, source_target_pairs={{8,0},{16,8},{24,16},{32,24},{40,32},{48,40},{56,48},{9,1},{17,9},... | collective-permute-start | bytes 417800 | tf_op jit(solution)/shard_map/ppermute | solution.py:409
  81.1 5.5 %shard_map.73.acc = f32[4,272,1024]{2,1,0:T(8,128)S(1)} custom-call(s32[3]{0:T(128)S(1)} %pad_add_fusion.sc, bf16[4,272,256]{2,1,0:T(8,128)(2,1)S(1)} %get-tuple-element.22.h, bf16[4608,1024]{1,0:T(8,128)(2,1)S(1)} %bitcast.57), custom_call_target="tpu_custom_call" | custom-call | flops 4058744064 | bytes 1048576 | tf_op jit(solution)/shard_map/pallas_call | solution.py:26
  86.7 0.1 pad_maximum_fusion
  86.9 1.9 %shard_map.74.acc = f32[4,272,1024]{2,1,0:T(8,128)S(1)} custom-call(s32[3]{0:T(128)S(1)} %pad_add_fusion.sc, bf16[272,256]{1,0:T(8,128)(2,1)S(1)} %collective-permute-done.7.top, bf16[272,256]{1,0:T(8,128)(2,1)S(1)} %collective-permute-done.8.bot, bf16[4608,1024]{1,0:T(8,128)(2,1)S(1)} %bitcast.60, ...), custom_call_target="tpu_custom_call", output_to_operand_aliasing={{}: (4, {})} | custom-call | flops 773094144 | bytes 1048576 | tf_op jit(solution)/shard_map/pallas_call | solution.py:26
  88.9 2.3 %collective-permute-done.9.recv = bf16[6,272,256]{2,1,0:T(8,128)(2,1)S(1)} collective-permute-done((bf16[6,272,256]{2,1,0:T(8,128)(2,1)S(1)}, bf16[6,272,256]{2,1,0:T(8,128)(2,1)S(1)}, u32[]{:S(2)}, u32[]{:S(2)}) %collective-permute-start.9) | collective-permute-done | bytes 835616 | tf_op jit(solution)/shard_map/ppermute | solution.py:427
  91.2 8.7 %shard_map.75 = (f32[4,272,1024]{2,1,0:T(8,128)S(1)}, bf16[1,4,256,256]{3,2,1,0:T(8,128)(2,1)}, f32[1,4,256,256]{3,2,1,0:T(8,128)}) custom-call(s32[3]{0:T(128)S(1)} %pad_add_fusion.sc, bf16[6,272,256]{2,1,0:T(8,128)(2,1)S(1)} %collective-permute-done.9.recv, bf16[4,272,256]{2,1,0:T(8,128)(2,1)S(1)} %get-tuple-element.22.h, ...), custom_call_target="tpu_custom_call", output_to_operand_aliasing={{0}: (6, {})} | custom-call | flops 4831838208 | bytes 1048576 | tf_op jit(solution)/shard_map/pallas_call | solution.py:26
  (54 shorter events, 0.5 us)
Async XLA Ops:
  0.6 13.5 %copy-start.6 = (bf16[1,4,256,256]{3,2,1,0:T(8,128)(2,1)S(1)}, bf16[1,4,256,256]{3,2,1,0:T(8,128)(2,1)}, u32[]{:S(2)}) copy-start(bf16[1,4,256,256]{3,2,1,0:T(8,128)(2,1)} %hid.3) | copy-start | bytes 1572868
  0.6 13.5 %copy-start.4 = (bf16[2,4,256,256]{3,2,1,0:T(8,128)(2,1)S(1)}, bf16[2,4,256,256]{3,2,1,0:T(8,128)(2,1)}, u32[]{:S(2)}) copy-start(bf16[2,4,256,256]{3,2,1,0:T(8,128)(2,1)} %fr.5) | copy-start | bytes 3145732
  3.6 19.2 %collective-permute-start = (bf16[3,256,256]{2,1,0:T(8,128)(2,1)}, bf16[3,256,256]{2,1,0:T(8,128)(2,1)S(1)}, u32[]{:S(2)}, u32[]{:S(2)}) collective-permute-start(bf16[3,256,256]{2,1,0:T(8,128)(2,1)} %pad_maximum_fusion.1), channel_id=1, source_target_pairs={{0,8},{8,16},{16,24},{24,32},{32,40},{40,48},{48,56},{1,9},{9,17},... | collective-permute-start | bytes 1179656 | tf_op jit(solution)/shard_map/ppermute | solution.py:335
  7.2 23.5 %slice-start = ((s8[9437184]{0:T(1024)(128)(4,1)}), s8[1048576]{0:T(1024)(128)(4,1)S(1)}, s32[]{:S(2)}) async-start(s8[9437184]{0:T(1024)(128)(4,1)} %bitcast.51), calls=%async_computation | async-start | bytes 2097152
  8.0 14.9 %collective-permute-start.1 = (bf16[3,256,256]{2,1,0:T(8,128)(2,1)}, bf16[3,256,256]{2,1,0:T(8,128)(2,1)S(1)}, u32[]{:S(2)}, u32[]{:S(2)}) collective-permute-start(bf16[3,256,256]{2,1,0:T(8,128)(2,1)} %pad_maximum_fusion.2), channel_id=1, source_target_pairs={{8,0},{16,8},{24,16},{32,24},{40,32},{48,40},{56,48},{9,1},{17,9},... | collective-permute-start | bytes 1179656 | tf_op jit(solution)/shard_map/ppermute | solution.py:336
  14.1 3.7 %copy-start = (bf16[1,4608,1024]{2,1,0:T(8,128)(2,1)S(1)}, bf16[1,4608,1024]{2,1,0:T(8,128)(2,1)}, u32[]{:S(2)}) copy-start(bf16[1,4608,1024]{2,1,0:T(8,128)(2,1)} %param.8) | copy-start | bytes 28311556
  17.8 12.9 %slice-start.1 = ((s8[9437184]{0:T(1024)(128)(4,1)}), s8[4194304]{0:T(1024)(128)(4,1)S(1)}, s32[]{:S(2)}) async-start(s8[9437184]{0:T(1024)(128)(4,1)} %bitcast.51), calls=%async_computation.1 | async-start | bytes 8388608
  17.8 12.9 %slice-start.2 = ((s8[9437184]{0:T(1024)(128)(4,1)}), s8[4194304]{0:T(1024)(128)(4,1)S(1)}, s32[]{:S(2)}) async-start(s8[9437184]{0:T(1024)(128)(4,1)} %bitcast.51), calls=%async_computation.2 | async-start | bytes 8388608
  23.0 9.8 %collective-permute-start.2 = (bf16[26,8,256]{2,1,0:T(8,128)(2,1)S(1)}, bf16[26,8,256]{2,1,0:T(8,128)(2,1)S(1)}, u32[]{:S(2)}, u32[]{:S(2)}) collective-permute-start(bf16[26,8,256]{2,1,0:T(8,128)(2,1)S(1)} %pad_maximum_fusion.3), channel_id=1, source_target_pairs={{0,1},{1,2},{2,3},{3,4},{4,5},{5,6},{6,7},{8,9},{9,10},{10,11},{11... | collective-permute-start | bytes 319496 | tf_op jit(solution)/shard_map/ppermute | solution.py:360
  27.2 7.0 %collective-permute-start.3 = (bf16[26,8,256]{2,1,0:T(8,128)(2,1)S(1)}, bf16[26,8,256]{2,1,0:T(8,128)(2,1)S(1)}, u32[]{:S(2)}, u32[]{:S(2)}) collective-permute-start(bf16[26,8,256]{2,1,0:T(8,128)(2,1)S(1)} %pad_maximum_fusion.4), channel_id=1, source_target_pairs={{1,0},{2,1},{3,2},{4,3},{5,4},{6,5},{7,6},{9,8},{10,9},{11,10},{12... | collective-permute-start | bytes 319496 | tf_op jit(solution)/shard_map/ppermute | solution.py:361
  30.7 3.5 %copy-start.5 = (f32[1,4,256,256]{3,2,1,0:T(8,128)S(1)}, f32[1,4,256,256]{3,2,1,0:T(8,128)}, u32[]{:S(2)}) copy-start(f32[1,4,256,256]{3,2,1,0:T(8,128)} %cell.1) | copy-start | bytes 3145732
  30.7 3.5 %copy-start.7 = (bf16[1,4,256,256]{3,2,1,0:T(8,128)(2,1)S(1)}, bf16[1,4,256,256]{3,2,1,0:T(8,128)(2,1)}, u32[]{:S(2)}) copy-start(bf16[1,4,256,256]{3,2,1,0:T(8,128)(2,1)} %hid.3) | copy-start | bytes 1572868
  30.7 3.5 %copy-start.10 = (f32[2,1024]{1,0:T(2,128)S(1)}, f32[2,1024]{1,0:T(2,128)}, u32[]{:S(2)}) copy-start(f32[2,1024]{1,0:T(2,128)} %bias.5) | copy-start | bytes 24580
  35.9 2.1 %copy-start.2 = (f32[4,272,1024]{2,1,0:T(8,128)}, f32[4,272,1024]{2,1,0:T(8,128)S(1)}, u32[]{:S(2)}) copy-start(f32[4,272,1024]{2,1,0:T(8,128)S(1)} %get-tuple-element.21.acc_b) | copy-start | bytes 13369348
  37.9 1.0 %copy-start.8 = (f32[4,272,256]{2,1,0:T(8,128)}, f32[4,272,256]{2,1,0:T(8,128)S(1)}, u32[]{:S(2)}) copy-start(f32[4,272,256]{2,1,0:T(8,128)S(1)} %get-tuple-element.20.cx) | copy-start | bytes 3342340
  39.0 14.2 %collective-permute-start.4 = (bf16[4,272,256]{2,1,0:T(8,128)(2,1)S(1)}, bf16[4,272,256]{2,1,0:T(8,128)(2,1)S(1)}, u32[]{:S(2)}, u32[]{:S(2)}) collective-permute-start(bf16[4,272,256]{2,1,0:T(8,128)(2,1)S(1)} %get-tuple-element.19.h), channel_id=1, source_target_pairs={{0,64},{64,0},{1,65},{65,1},{2,66},{66,2},{3,67},{67,3},{4,68},{68... | collective-permute-start | bytes 1671176 | tf_op jit(solution)/shard_map/ppermute | solution.py:387
  53.2 17.1 %collective-permute-start.6 = (bf16[272,256]{1,0:T(8,128)(2,1)S(1)}, bf16[272,256]{1,0:T(8,128)(2,1)S(1)}, u32[]{:S(2)}, u32[]{:S(2)}) collective-permute-start(bf16[272,256]{1,0:T(8,128)(2,1)S(1)} %get-tuple-element.36), channel_id=1, source_target_pairs={{8,0},{16,8},{24,16},{32,24},{40,32},{48,40},{56,48},{9,1},{17,9},... | collective-permute-start | bytes 417800 | tf_op jit(solution)/shard_map/ppermute | solution.py:390
  56.7 13.7 %collective-permute-start.5 = (bf16[272,256]{1,0:T(8,128)(2,1)S(1)}, bf16[272,256]{1,0:T(8,128)(2,1)S(1)}, u32[]{:S(2)}, u32[]{:S(2)}) collective-permute-start(bf16[272,256]{1,0:T(8,128)(2,1)S(1)} %get-tuple-element.37), channel_id=1, source_target_pairs={{0,8},{8,16},{16,24},{24,32},{32,40},{40,48},{48,56},{1,9},{9,17},... | collective-permute-start | bytes 417800 | tf_op jit(solution)/shard_map/ppermute | solution.py:389
  58.6 3.7 %copy-start.1 = (bf16[1,4608,1024]{2,1,0:T(8,128)(2,1)S(1)}, bf16[1,4608,1024]{2,1,0:T(8,128)(2,1)}, u32[]{:S(2)}) copy-start(bf16[1,4608,1024]{2,1,0:T(8,128)(2,1)} %param.8) | copy-start | bytes 28311556
  62.3 2.3 %copy-start.3 = (f32[4,272,1024]{2,1,0:T(8,128)S(1)}, f32[4,272,1024]{2,1,0:T(8,128)}, u32[]{:S(2)}) copy-start(f32[4,272,1024]{2,1,0:T(8,128)} %copy-done.2) | copy-start | bytes 13369348
  64.6 5.8 %copy-start.9 = (f32[4,272,256]{2,1,0:T(8,128)S(1)}, f32[4,272,256]{2,1,0:T(8,128)}, u32[]{:S(2)}) copy-start(f32[4,272,256]{2,1,0:T(8,128)} %copy-done.8) | copy-start | bytes 3342340
  70.4 16.4 %slice-start.3 = ((s8[9437184]{0:T(1024)(128)(4,1)}), s8[1048576]{0:T(1024)(128)(4,1)S(1)}, s32[]{:S(2)}) async-start(s8[9437184]{0:T(1024)(128)(4,1)} %bitcast.58), calls=%async_computation.3 | async-start | bytes 2097152
  70.4 16.4 %slice-start.4 = ((s8[9437184]{0:T(1024)(128)(4,1)}), s8[4194304]{0:T(1024)(128)(4,1)S(1)}, s32[]{:S(2)}) async-start(s8[9437184]{0:T(1024)(128)(4,1)} %bitcast.58), calls=%async_computation.4 | async-start | bytes 8388608
  73.4 13.2 %collective-permute-start.7 = (bf16[272,256]{1,0:T(8,128)(2,1)S(1)}, bf16[272,256]{1,0:T(8,128)(2,1)S(1)}, u32[]{:S(2)}, u32[]{:S(2)}) collective-permute-start(bf16[272,256]{1,0:T(8,128)(2,1)S(1)} %get-tuple-element.34), channel_id=1, source_target_pairs={{0,8},{8,16},{16,24},{24,32},{32,40},{40,48},{48,56},{1,9},{9,17},... | collective-permute-start | bytes 417800 | tf_op jit(solution)/shard_map/ppermute | solution.py:408
  75.4 11.5 %slice-start.5 = ((s8[9437184]{0:T(1024)(128)(4,1)}), s8[4194304]{0:T(1024)(128)(4,1)S(1)}, s32[]{:S(2)}) async-start(s8[9437184]{0:T(1024)(128)(4,1)} %bitcast.58), calls=%async_computation.5 | async-start | bytes 8388608
  75.4 11.3 %collective-permute-start.8 = (bf16[272,256]{1,0:T(8,128)(2,1)S(1)}, bf16[272,256]{1,0:T(8,128)(2,1)S(1)}, u32[]{:S(2)}, u32[]{:S(2)}) collective-permute-start(bf16[272,256]{1,0:T(8,128)(2,1)S(1)} %get-tuple-element.35), channel_id=1, source_target_pairs={{8,0},{16,8},{24,16},{32,24},{40,32},{48,40},{56,48},{9,1},{17,9},... | collective-permute-start | bytes 417800 | tf_op jit(solution)/shard_map/ppermute | solution.py:409
  88.8 2.4 %collective-permute-start.9 = (bf16[6,272,256]{2,1,0:T(8,128)(2,1)S(1)}, bf16[6,272,256]{2,1,0:T(8,128)(2,1)S(1)}, u32[]{:S(2)}, u32[]{:S(2)}) collective-permute-start(bf16[6,272,256]{2,1,0:T(8,128)(2,1)S(1)} %pad_maximum_fusion), channel_id=1, source_target_pairs={{0,64},{64,0},{1,65},{65,1},{2,66},{66,2},{3,67},{67,3},{4,68},{68... | collective-permute-start | bytes 2506760 | tf_op jit(solution)/shard_map/ppermute | solution.py:427

commit v2 on v0

v2 whole, which is shorter than its diff:
```python
import jax
import jax.numpy as jnp
from jax import lax
from jax.experimental import pallas as pl
from jax.experimental.pallas import tpu as pltpu
from jax.sharding import PartitionSpec as P

f32 = jnp.float32
bf16 = jnp.bfloat16
ROWS, COLS, CH, GATES = 4, 256, 256, 1024
PAD = 8
EXT = COLS + 2 * PAD
LO, HI = 16, EXT - 16
NB = 512
UNIT = 2 * ROWS * COLS * 4608 * 1024
ACC = (ROWS, EXT, GATES)
TILE = (ROWS, EXT, CH)
STACK = (3, ROWS, EXT, CH)
PAIR = (3, 2, EXT, CH)
EDGE = (20, PAD, CH)

ANYV = pl.BlockSpec(memory_space=pltpu.VMEM)


def vm(shape, dtype):
    return pltpu.VMEM(shape, dtype)


def call(body, outs, args, aliases=None, scratch=(), part=0.0, limit=8):
    return pl.pallas_call(
        body,
        in_specs=[ANYV] * len(args),
        out_specs=[ANYV] * len(outs),
        out_shape=list(outs),
        scratch_shapes=list(scratch),
        input_output_aliases=aliases or {},
        compiler_params=pltpu.CompilerParams(vmem_limit_bytes=limit << 20),
        cost_estimate=pl.CostEstimate(flops=int(UNIT * part), bytes_accessed=1 << 20, transcendentals=0),
    )(*args)


def core_is(k):
    return pl.when(lax.axis_index("layer") == k)


def inside(axis, step):
    at = lax.axis_index(axis) + step
    return jnp.logical_and(at >= 0, at < lax.axis_size(axis)).astype(f32)


def build(stack, r, x):
    x = x.astype(f32)
    stack[0, r] = pltpu.roll(x, 1, 0).astype(bf16)
    stack[1, r] = x.astype(bf16)
    stack[2, r] = pltpu.roll(x, EXT - 1, 0).astype(bf16)


def widen(row, left, right):
    a = left.astype(f32) * inside("gx", -1)
    b = right.astype(f32) * inside("gx", 1)
    return jnp.concatenate([a, row.astype(f32), b], axis=0)


def bare(row):
    zero = jnp.zeros((PAD, CH), f32)
    return jnp.concatenate([zero, row.astype(f32), zero], axis=0)


def columns(body):
    def step(n, carry):
        body(pl.ds(pl.multiple_of(n * NB, NB), NB))
        return carry

    lax.fori_loop(0, GATES // NB, step, 0)


def taps(w, c, lhs, off, tap, total):
    d = jnp.dot(lhs, w[pl.ds(tap * 512 + off, 256), c], preferred_element_type=f32)
    return d if total is None else total + d


def inner(acc, w, stack, off, c, lo, hi, add):
    for r in range(ROWS):
        total = acc[r, lo:hi, c] if add else None
        for dy in range(3):
            q = r + dy - 1
            if 0 <= q < ROWS:
                for dx in range(3):
                    total = taps(w, c, stack[dx, q, lo:hi, :], off, 3 * dy + dx, total)
        acc[r, lo:hi, c] = total


def outer(acc, w, parts, c):
    for r, q, dy in ((0, 0, 0), (ROWS - 1, 1, 2)):
        total = acc[r, :, c]
        for dx in range(3):
            for stack, off in parts:
                total = taps(w, c, stack[dx, q], off, 3 * dy + dx, total)
        acc[r, :, c] = total


def sigmoid(x):
    return 0.5 * jnp.tanh(0.5 * x) + 0.5


def gates_at(acc, b, r, at, cell):
    g = [acc[r, at, i * CH : (i + 1) * CH] + b[:, i * CH : (i + 1) * CH] for i in range(4)]
    cell = sigmoid(g[1]) * cell + sigmoid(g[0]) * jnp.tanh(g[3])
    return cell, sigmoid(g[2]) * jnp.tanh(cell)


def epilogue(acc, bias, layer, cell_in, cell_out, h):
    b = bias[layer : layer + 1, :]
    first = PAD * (1 - inside("gx", -1)).astype(jnp.int32)
    last = EXT - PAD * (1 - inside("gx", 1)).astype(jnp.int32)

    def step(k, carry):
        at = pl.ds(pl.multiple_of(k * 16, 16), 16)
        col = lax.broadcasted_iota(jnp.int32, (16, CH), 0) + k * 16
        keep = jnp.logical_and(col >= first, col < last)
        for r in range(ROWS):
            new, hid = gates_at(acc, b, r, at, cell_in[r, at])
            cell_out[r, at] = new
            h[r, at] = jnp.where(keep, hid, 0.0).astype(bf16)
        return carry

    lax.fori_loop(0, EXT // 16, step, 0)


def k_edges(fr, hid, cell, to_left, to_right):
    for out, a in ((to_left, 0), (to_right, COLS - PAD)):
        for r in range(ROWS):
            out[r] = fr[0, r, a : a + PAD]
            out[4 + r] = fr[1, r, a : a + PAD]
            out[8 + r] = hid[0, r, a : a + PAD]
            c = cell[0, r, a : a + PAD]
            hi = c.astype(bf16)
            out[12 + r] = hi
            out[16 + r] = (c - hi.astype(f32)).astype(bf16)


def k_hidden(hid, w, acc, s):
    for r in range(ROWS):
        build(s, r, bare(hid[0, r]))
    columns(lambda c: inner(acc, w, s, 256, c, LO, HI, False))


def k_rows(fr, hid, left, right, up, down):
    for out, r in ((up, 0), (down, ROWS - 1)):
        for i in range(3):
            row = hid[0, r] if i == 2 else fr[i, r]
            out[i] = widen(row, left[4 * i + r], right[4 * i + r]).astype(bf16)


def k_frames(fr, hid, cell, w, left, right, acc_in, acc, acc_b, cx, s, t):
    for r in range(ROWS):
        a = left[12 + r].astype(f32) + left[16 + r].astype(f32)
        b = right[12 + r].astype(f32) + right[16 + r].astype(f32)
        cx[r] = jnp.concatenate([a, cell[0, r], b], axis=0)
        x = widen(hid[0, r], left[8 + r], right[8 + r])
        for dx, y in ((0, pltpu.roll(x, 1, 0)), (1, x), (2, pltpu.roll(x, EXT - 1, 0))):
            t[dx, r, 0:16] = y[0:16].astype(bf16)
            t[dx, r, 16:32] = y[HI:EXT].astype(bf16)

    def sides(c):
        total = None
        for dy in range(3):
            n = ROWS if dy == 1 else ROWS - 1
            first = max(dy - 1, 0)
            for dx in range(3):
                lhs = t[dx, first : first + n].reshape(n * 32, CH)
                d = jnp.dot(lhs, w[pl.ds((3 * dy + dx) * 512 + 256, 256), c], preferred_element_type=f32)
                zero = jnp.zeros((32, NB), f32)
                if dy == 0:
                    d = jnp.concatenate([zero, d], axis=0)
                if dy == 2:
                    d = jnp.concatenate([d, zero], axis=0)
                total = d if total is None else total + d
        for r in range(ROWS):
            acc[r, 0:LO, c] = total[r * 32 : r * 32 + 16]
            acc[r, HI:EXT, c] = total[r * 32 + 16 : r * 32 + 32]

    columns(sides)

    @core_is(0)
    def _():
        for r in range(ROWS):
            build(s, r, widen(fr[0, r], left[r], right[r]))
        columns(lambda c: inner(acc, w, s, 0, c, 0, EXT, True))
        for r in range(ROWS):
            build(s, r, widen(fr[1, r], left[4 + r], right[4 + r]))
        columns(lambda c: inner(acc_b, w, s, 0, c, 0, EXT, False))


def halo(s, top, bot):
    build(s, 0, top.astype(f32) * inside("gy", -1))
    build(s, 1, bot.astype(f32) * inside("gy", 1))


def k_first(top, bot, w, bias, cx_in, acc_in, acc, h, cx, s):
    halo(s.at[1], top[2], bot[2])

    @core_is(0)
    def _():
        halo(s.at[0], top[0], bot[0])
        columns(lambda c: outer(acc, w, ((s.at[0], 0), (s.at[1], 256)), c))
        epilogue(acc, bias, 0, cx, cx, h)

    @core_is(1)
    def _():
        columns(lambda c: outer(acc, w, ((s.at[1], 256),), c))


def k_second(top, bot, w, acc_in, acc, s):
    @core_is(0)
    def _():
        halo(s, top[1], bot[1])
        columns(lambda c: outer(acc, w, ((s, 0),), c))


def k_pick(h, recv, up, down):
    @core_is(0)
    def _():
        up[...] = h[0]
        down[...] = h[ROWS - 1]

    @core_is(1)
    def _():
        up[...] = recv[0]
        down[...] = recv[ROWS - 1]


def k_third(h, recv, w, a_in, b_in, acc_a, acc_b, s):
    @core_is(0)
    def _():
        for r in range(ROWS):
            build(s, r, h[r])
        columns(lambda c: inner(acc_b, w, s, 256, c, 0, EXT, True))

    @core_is(1)
    def _():
        for r in range(ROWS):
            build(s, r, recv[r])
        columns(lambda c: inner(acc_a, w, s, 0, c, 0, EXT, True))


def k_fourth(top, bot, w, bias, cx_in, a_in, b_in, acc_a, acc_b, cx, h, up, down, s):
    halo(s, top[...], bot[...])

    @core_is(0)
    def _():
        columns(lambda c: outer(acc_b, w, ((s, 256),), c))
        epilogue(acc_b, bias, 0, cx, cx, h)

    @core_is(1)
    def _():
        columns(lambda c: outer(acc_a, w, ((s, 0),), c))
        epilogue(acc_a, bias, 1, cx, cx, h)

    up[...] = h[0]
    down[...] = h[ROWS - 1]


def k_fifth(h, w, acc_in, acc, s):
    @core_is(1)
    def _():
        for r in range(ROWS):
            build(s, r, h[r])
        columns(lambda c: inner(acc, w, s, 256, c, 0, EXT, False))


def k_sixth(top, bot, w, acc_in, acc, out, s):
    @core_is(0)
    def _():
        out[0] = top[...]
        out[1] = bot[...]

    @core_is(1)
    def _():
        halo(s, top[...], bot[...])
        columns(lambda c: outer(acc, w, ((s, 256),), c))


def k_seventh(recv, w, acc_in, acc, s):
    @core_is(1)
    def _():
        for r in range(ROWS):
            build(s, r, recv[r])
        columns(lambda c: inner(acc, w, s, 0, c, 0, EXT, True))


def k_last(two, h, cx, w, bias, acc_in, acc, ho, co, s):
    @core_is(0)
    def _():
        for r in range(ROWS):
            ho[0, r] = h[r].astype(f32)[PAD : PAD + COLS].astype(bf16)
            co[0, r] = cx[r, PAD : PAD + COLS]

    @core_is(1)
    def _():
        halo(s, two[0], two[1])
        columns(lambda c: outer(acc, w, ((s, 0),), c))
        b = bias[1:2, :]

        def step(k, carry):
            at = pl.ds(pl.multiple_of(k * 16, 16), 16)
            src = pl.ds(pl.multiple_of(k * 16 + PAD, 8), 16)
            for r in range(ROWS):
                new, hid = gates_at(acc, b, r, src, cx[r, src])
                co[0, r, at] = new
                ho[0, r, at] = hid.astype(bf16)
            return carry

        lax.fori_loop(0, COLS // 16, step, 0)


def both_ways(axis, to_low, to_high):
    n = lax.axis_size(axis)
    from_low = lax.ppermute(to_high, axis, [(i, (i + 1) % n) for i in range(n)])
    from_high = lax.ppermute(to_low, axis, [(i, (i - 1) % n) for i in range(n)])
    return from_low, from_high


def per_device(frames, hidden_init, cell_init, conv_weight, conv_bias):
    w = pltpu.with_memory_space_constraint(conv_weight[0], pltpu.VMEM)
    bias = conv_bias
    swap = [(0, 1), (1, 0)]

    edge = vm(EDGE, bf16)
    to_left, to_right = call(k_edges, [edge, edge], [frames, hidden_init, cell_init])
    left, right = both_ways("gx", to_left, to_right)
    (acc_a,) = call(k_hidden, [vm(ACC, f32)], [hidden_init, w], scratch=[pltpu.VMEM(STACK, bf16)], part=0.4)

    rows = vm((3, EXT, CH), bf16)
    to_up, to_down = call(k_rows, [rows, rows], [frames, hidden_init, left, right])
    top, bot = both_ways("gy", to_up, to_down)
    acc_a, acc_b, cx = call(
        k_frames,
        [vm(ACC, f32), vm(ACC, f32), vm(TILE, f32)],
        [frames, hidden_init, cell_init, w, left, right, acc_a],
        aliases={6: 0},
        scratch=[pltpu.VMEM(STACK, bf16), pltpu.VMEM((3, ROWS, 32, CH), bf16)],
        part=0.95,
    )
    acc_a, h, cx = call(
        k_first,
        [vm(ACC, f32), vm(TILE, bf16), vm(TILE, f32)],
        [top, bot, w, bias, cx, acc_a],
        aliases={5: 0, 4: 2},
        scratch=[pltpu.VMEM((2,) + PAIR, bf16)],
        part=0.3,
    )

    recv = lax.ppermute(h, "layer", swap)
    (acc_b,) = call(
        k_second, [vm(ACC, f32)], [top, bot, w, acc_b], aliases={3: 0}, scratch=[pltpu.VMEM(PAIR, bf16)], part=0.1
    )
    row = vm((EXT, CH), bf16)
    to_up, to_down = call(k_pick, [row, row], [h, recv])
    top, bot = both_ways("gy", to_up, to_down)
    acc_a, acc_b = call(
        k_third,
        [vm(ACC, f32), vm(ACC, f32)],
        [h, recv, w, acc_a, acc_b],
        aliases={3: 0, 4: 1},
        scratch=[pltpu.VMEM(STACK, bf16)],
        part=0.45,
    )
    acc_a, acc_b, cx, h, to_up, to_down = call(
        k_fourth,
        [vm(ACC, f32), vm(ACC, f32), vm(TILE, f32), vm(TILE, bf16), row, row],
        [top, bot, w, bias, cx, acc_a, acc_b],
        aliases={4: 2, 5: 0, 6: 1},
        scratch=[pltpu.VMEM(PAIR, bf16)],
        part=0.3,
    )

    top, bot = both_ways("gy", to_up, to_down)
    recv = lax.ppermute(h, "layer", swap)
    (acc_b,) = call(
        k_fifth, [vm(ACC, f32)], [h, w, acc_b], aliases={2: 0}, scratch=[pltpu.VMEM(STACK, bf16)], part=0.45
    )
    acc_b, two = call(
        k_sixth,
        [vm(ACC, f32), vm((2, EXT, CH), bf16)],
        [top, bot, w, acc_b],
        aliases={3: 0},
        scratch=[pltpu.VMEM(PAIR, bf16)],
        part=0.1,
    )
    two = lax.ppermute(two, "layer", swap)
    (acc_b,) = call(
        k_seventh, [vm(ACC, f32)], [recv, w, acc_b], aliases={2: 0}, scratch=[pltpu.VMEM(STACK, bf16)], part=0.45
    )
    _, ho, co = call(
        k_last,
        [
            vm(ACC, f32),
            jax.ShapeDtypeStruct((1, ROWS, COLS, CH), bf16),
            jax.ShapeDtypeStruct((1, ROWS, COLS, CH), f32),
        ],
        [two, h, cx, w, bias, acc_b],
        aliases={5: 0},
        scratch=[pltpu.VMEM(PAIR, bf16)],
        part=0.3,
    )
    return ho, co


def solution(mesh):
    placed = (
        P(None, "gy", "gx", None),
        P("layer", "gy", "gx", None),
        P("layer", "gy", "gx", None),
        P("layer", None, None),
        P(),
    )
    return jax.shard_map(
        per_device,
        mesh=mesh,
        in_specs=placed,
        out_specs=(P("layer", "gy", "gx", None), P("layer", "gy", "gx", None)),
        check_vma=False,
    )
```

time: 201 us -> 73.3 us (0.36); the launches traced: 198 us -> 73 us
  matrix products: 107 us -> 0 us
  Pallas kernels: 0 us -> 29.4 us
  other arithmetic: 19.3 us -> 0 us
  waiting for transfers between devices: 27 us -> 9.1 us
  starting transfers between devices: 40.9 us -> 25.5 us
  local copies, waits for them, and re-layouts: 3.24 us -> 8.22 us
    dot_general x27 -> x0, matrix products: 107 us -> none  [tile_gates(): jnp.dot(window, kernel[tap * width:(tap + 1) * width], preferred_element_...]
    pallas_call x0 -> x13, Pallas kernels: none -> 29.4 us  [call(): pl.pallas_call(body, in_specs=[ANYV] * len(args), out_specs=[ANYV] * len(...]
    ppermute x14 -> x11, waiting for transfers between devices: 27 us -> 9.1 us  [the longest x4 7.51 us: both_ways(): from_low = lax.ppermute(to_high, axis, [(i, (i + 1) % n) for i in range(n)])]
    ppermute x14 -> x11, starting transfers between devices: 40.9 us -> 25.5 us  [the longest x4 12.5 us: both_ways(): from_high = lax.ppermute(to_low, axis, [(i, (i - 1) % n) for i in range(n)])]
    concatenate x11 -> x0, other arithmetic: 8.59 us -> none  [the longest x9 7.73 us: extended(): block = jnp.concatenate([low, block, high], axis=dim)]
    unnamed x28 -> x20, local copies, waits for them, and re-layouts: 0.09 us -> 8.22 us
    select_n x6 -> x0, other arithmetic: 6.82 us -> none  [the longest x2 4.54 us: per_device(): hidden = jnp.where(active, new_hidden, hidden)]
    slice x5 -> x0, local copies, waits for them, and re-layouts: 3.14 us -> none  [tile_gates(): padded[tap // 3:tap // 3 + rows, tap % 3:tap % 3 + cols, :]]
  transfers between devices with their start and end apart: 14 -> 11, of which waited for: 7 -> 2; matrix products, arithmetic and copies ran while one was open for 15% -> 0% of each run, Pallas kernels for 0% -> 30%
where the time goes in v2:
time: 73.3 us; the launch traced here: 73 us
  Pallas kernels  29.4 us (40%)
  starting transfers between devices  25.5 us (35%)
  waiting for transfers between devices  9.1 us (12%)
  local copies, waits for them, and re-layouts  8.22 us (11%)
  between operations  0.82 us (1%)
    pallas_call x13, Pallas kernels, call(): pl.pallas_call(body, in_specs=[ANYV] * len(args), out_specs=[ANYV] * len(...  29.4 us
    ppermute x4, starting transfers between devices, both_ways(): from_high = lax.ppermute(to_low, axis, [(i, (i - 1) % n) for i in range(n)])  12.5 us
    unnamed x20, local copies, waits for them, and re-layouts  8.22 us
    ppermute x4, waiting for transfers between devices, both_ways(): from_low = lax.ppermute(to_high, axis, [(i, (i + 1) % n) for i in range(n)])  7.51 us
    ppermute x2, starting transfers between devices, per_device(): recv = lax.ppermute(h, 'layer', swap)  7.26 us
    ppermute x4, starting transfers between devices, both_ways(): from_low = lax.ppermute(to_high, axis, [(i, (i + 1) % n) for i in range(n)])  5.6 us
    ppermute x2, waiting for transfers between devices, per_device(): recv = lax.ppermute(h, 'layer', swap)  1.59 us
  transfers between devices with their start and end apart: 11, of which 2 were waited for; matrix products, arithmetic and copies ran while one was open for 0% of the time, Pallas kernels for 30%

profile of v2, /device:TPU:1, one launch (start us, length us, event | category | flops | bytes accessed | tf_op | source)
XLA Modules:
  0.0 73.0 jit_solution(18043997612692693377)
XLA Ops:
  0.6 0.0 copy-start.2
  0.6 1.0 %copy-done.2 = bf16[1,4,256,256]{3,2,1,0:T(8,128)(2,1)S(1)} copy-done((bf16[1,4,256,256]{3,2,1,0:T(8,128)(2,1)S(1)}, bf16[1,4,256,256]{3,2,1,0:T(8,128)(2,1)}, u32[]{:S(2)}) %copy-start.2) | copy-done | bytes 524312
  1.7 1.2 %copy-done.5 = bf16[2,4,256,256]{3,2,1,0:T(8,128)(2,1)S(1)} copy-done((bf16[2,4,256,256]{3,2,1,0:T(8,128)(2,1)S(1)}, bf16[2,4,256,256]{3,2,1,0:T(8,128)(2,1)}, u32[]{:S(2)}) %copy-start.5) | copy-done | bytes 1048600
  2.9 1.2 %copy-done.7 = f32[1,4,256,256]{3,2,1,0:T(8,128)S(1)} copy-done((f32[1,4,256,256]{3,2,1,0:T(8,128)S(1)}, f32[1,4,256,256]{3,2,1,0:T(8,128)}, u32[]{:S(2)}) %copy-start.7) | copy-done | bytes 1048600
  4.1 3.8 %collective-permute-start = (bf16[20,8,256]{2,1,0:T(8,128)(2,1)S(1)}, bf16[20,8,256]{2,1,0:T(8,128)(2,1)S(1)}, u32[]{:S(2)}, u32[]{:S(2)}) collective-permute-start(bf16[20,8,256]{2,1,0:T(8,128)(2,1)S(1)} %get-tuple-element.25), channel_id=1, source_target_pairs={{0,1},{1,2},{2,3},{3,4},{4,5},{5,6},{6,7},{7,0},{8,9},{9,10},{10,1... | collective-permute-start | bytes 245768 | tf_op jit(solution)/shard_map/ppermute | solution.py:319
  8.0 2.3 %collective-permute-start.1 = (bf16[20,8,256]{2,1,0:T(8,128)(2,1)S(1)}, bf16[20,8,256]{2,1,0:T(8,128)(2,1)S(1)}, u32[]{:S(2)}, u32[]{:S(2)}) collective-permute-start(bf16[20,8,256]{2,1,0:T(8,128)(2,1)S(1)} %get-tuple-element.26), channel_id=1, source_target_pairs={{0,7},{1,0},{2,1},{3,2},{4,3},{5,4},{6,5},{7,6},{8,15},{9,8},{10,9... | collective-permute-start | bytes 245768 | tf_op jit(solution)/shard_map/ppermute | solution.py:320
  10.2 3.7 %copy-done = bf16[1,4608,1024]{2,1,0:T(8,128)(2,1)S(1)} copy-done((bf16[1,4608,1024]{2,1,0:T(8,128)(2,1)S(1)}, bf16[1,4608,1024]{2,1,0:T(8,128)(2,1)}, u32[]{:S(2)}) %copy-start) | copy-done | bytes 9437208
  13.9 1.0 %copy-done.3 = bf16[1,4,256,256]{3,2,1,0:T(8,128)(2,1)S(1)} copy-done((bf16[1,4,256,256]{3,2,1,0:T(8,128)(2,1)S(1)}, bf16[1,4,256,256]{3,2,1,0:T(8,128)(2,1)}, u32[]{:S(2)}) %copy-start.3) | copy-done | bytes 524312
  15.0 4.4 %shard_map.70.acc_in = f32[4,272,1024]{2,1,0:T(8,128)S(1)} custom-call(bf16[1,4,256,256]{3,2,1,0:T(8,128)(2,1)S(1)} %copy-done.3, bf16[4608,1024]{1,0:T(8,128)(2,1)S(1)} %bitcast.1), custom_call_target="tpu_custom_call" | custom-call | flops 3865470464 | bytes 1048576 | tf_op jit(solution)/shard_map/pallas_call | solution.py:30
  19.4 0.0 collective-permute-done.1.right
  19.4 0.1 shard_map.69
  19.5 1.7 %collective-permute-start.2 = (bf16[3,272,256]{2,1,0:T(8,128)(2,1)S(1)}, bf16[3,272,256]{2,1,0:T(8,128)(2,1)S(1)}, u32[]{:S(2)}, u32[]{:S(2)}) collective-permute-start(bf16[3,272,256]{2,1,0:T(8,128)(2,1)S(1)} %get-tuple-element.27), channel_id=1, source_target_pairs={{0,8},{8,16},{16,24},{24,32},{32,40},{40,48},{48,56},{56,0},{1,9},... | collective-permute-start | bytes 1253384 | tf_op jit(solution)/shard_map/ppermute | solution.py:319
  21.2 3.1 %collective-permute-start.3 = (bf16[3,272,256]{2,1,0:T(8,128)(2,1)S(1)}, bf16[3,272,256]{2,1,0:T(8,128)(2,1)S(1)}, u32[]{:S(2)}, u32[]{:S(2)}) collective-permute-start(bf16[3,272,256]{2,1,0:T(8,128)(2,1)S(1)} %get-tuple-element.28), channel_id=1, source_target_pairs={{0,56},{8,0},{16,8},{24,16},{32,24},{40,32},{48,40},{56,48},{1,57}... | collective-permute-start | bytes 1253384 | tf_op jit(solution)/shard_map/ppermute | solution.py:320
  24.3 1.1 %shard_map.71 = (f32[4,272,1024]{2,1,0:T(8,128)S(1)}, f32[4,272,1024]{2,1,0:T(8,128)S(1)}, f32[4,272,256]{2,1,0:T(8,128)S(1)}) custom-call(bf16[2,4,256,256]{3,2,1,0:T(8,128)(2,1)S(1)} %copy-done.6, bf16[1,4,256,256]{3,2,1,0:T(8,128)(2,1)S(1)} %copy-done.4, f32[1,4,256,256]{3,2,1,0:T(8,128)S(1)} %copy-done.8, ...), custom_call_target="tpu_custom_call", output_to_operand_aliasing={{0}: (6, {})} | custom-call | flops 9180492800 | bytes 1048576 | tf_op jit(solution)/shard_map/pallas_call | solution.py:30
  25.5 7.5 %collective-permute-done.2.top = bf16[3,272,256]{2,1,0:T(8,128)(2,1)S(1)} collective-permute-done((bf16[3,272,256]{2,1,0:T(8,128)(2,1)S(1)}, bf16[3,272,256]{2,1,0:T(8,128)(2,1)S(1)}, u32[]{:S(2)}, u32[]{:S(2)}) %collective-permute-start.2) | collective-permute-done | bytes 417824 | tf_op jit(solution)/shard_map/ppermute | solution.py:319
  33.0 0.0 collective-permute-done.3.bot
  33.0 1.4 %shard_map.72 = (f32[4,272,1024]{2,1,0:T(8,128)S(1)}, bf16[4,272,256]{2,1,0:T(8,128)(2,1)S(1)}, f32[4,272,256]{2,1,0:T(8,128)S(1)}) custom-call(bf16[3,272,256]{2,1,0:T(8,128)(2,1)S(1)} %collective-permute-done.2.top, bf16[3,272,256]{2,1,0:T(8,128)(2,1)S(1)} %collective-permute-done.3.bot, ...), custom_call_target="tpu_custom_call", output_to_operand_aliasing={{0}: (5, {}), {2}: (4, {})} | custom-call | flops 2899102976 | bytes 1048576 | tf_op jit(solution)/shard_map/pallas_call | solution.py:30
  34.3 6.2 %collective-permute-start.4 = (bf16[4,272,256]{2,1,0:T(8,128)(2,1)S(1)}, bf16[4,272,256]{2,1,0:T(8,128)(2,1)S(1)}, u32[]{:S(2)}, u32[]{:S(2)}) collective-permute-start(bf16[4,272,256]{2,1,0:T(8,128)(2,1)S(1)} %get-tuple-element.31.h), channel_id=1, source_target_pairs={{0,64},{64,0},{1,65},{65,1},{2,66},{66,2},{3,67},{67,3},{4,68},{68... | collective-permute-start | bytes 1671176 | tf_op jit(solution)/shard_map/ppermute | solution.py:354
  40.6 1.6 %collective-permute-done.4.recv = bf16[4,272,256]{2,1,0:T(8,128)(2,1)S(1)} collective-permute-done((bf16[4,272,256]{2,1,0:T(8,128)(2,1)S(1)}, bf16[4,272,256]{2,1,0:T(8,128)(2,1)S(1)}, u32[]{:S(2)}, u32[]{:S(2)}) %collective-permute-start.4) | collective-permute-done | bytes 557088 | tf_op jit(solution)/shard_map/ppermute | solution.py:354
  42.2 0.1 collective-permute-start.5
  42.3 3.6 %collective-permute-start.6 = (bf16[272,256]{1,0:T(8,128)(2,1)S(1)}, bf16[272,256]{1,0:T(8,128)(2,1)S(1)}, u32[]{:S(2)}, u32[]{:S(2)}) collective-permute-start(bf16[272,256]{1,0:T(8,128)(2,1)S(1)} %get-tuple-element.33), channel_id=1, source_target_pairs={{0,56},{8,0},{16,8},{24,16},{32,24},{40,32},{48,40},{56,48},{1,57}... | collective-permute-start | bytes 417800 | tf_op jit(solution)/shard_map/ppermute | solution.py:320
  45.8 5.0 %shard_map.75 = (f32[4,272,1024]{2,1,0:T(8,128)S(1)}, f32[4,272,1024]{2,1,0:T(8,128)S(1)}) custom-call(bf16[4,272,256]{2,1,0:T(8,128)(2,1)S(1)} %get-tuple-element.31.h, bf16[4,272,256]{2,1,0:T(8,128)(2,1)S(1)} %collective-permute-done.4.recv, bf16[4608,1024]{1,0:T(8,128)(2,1)S(1)} %bitcast.5, ...), custom_call_target="tpu_custom_call", output_to_operand_aliasing={{0}: (3, {}), {1}: (4, {})} | custom-call | flops 4348654592 | bytes 1048576 | tf_op jit(solution)/shard_map/pallas_call | solution.py:30
  50.8 0.0 collective-permute-done.5.top
  50.8 2.5 %shard_map.76 = (f32[4,272,1024]{2,1,0:T(8,128)S(1)}, f32[4,272,1024]{2,1,0:T(8,128)S(1)}, f32[4,272,256]{2,1,0:T(8,128)S(1)}, bf16[4,272,256]{2,1,0:T(8,128)(2,...) custom-call(bf16[272,256]{1,0:T(8,128)(2,1)S(1)} %collective-permute, ...), custom_call_target="tpu_custom_call", output_to_operand_aliasing={{2}: (4, {}), {0}: (5, {}), {1}: (6, {})} | custom-call | flops 2899102976 | bytes 1048576 | tf_op jit(solution)/shard_map/pallas_call | solution.py:30
  53.4 1.0 %collective-permute-start.10 = (bf16[4,272,256]{2,1,0:T(8,128)(2,1)S(1)}, bf16[4,272,256]{2,1,0:T(8,128)(2,1)S(1)}, u32[]{:S(2)}, u32[]{:S(2)}) collective-permute-start(bf16[4,272,256]{2,1,0:T(8,128)(2,1)S(1)} %get-tuple-element.41.h), channel_id=1, source_target_pairs={{0,64},{64,0},{1,65},{65,1},{2,66},{66,2},{3,67},{67,3},{4,68},{68... | collective-permute-start | bytes 1671176 | tf_op jit(solution)/shard_map/ppermute | solution.py:379
  54.4 3.6 %collective-permute-start.8 = (bf16[272,256]{1,0:T(8,128)(2,1)S(1)}, bf16[272,256]{1,0:T(8,128)(2,1)S(1)}, u32[]{:S(2)}, u32[]{:S(2)}) collective-permute-start(bf16[272,256]{1,0:T(8,128)(2,1)S(1)} %get-tuple-element.40), channel_id=1, source_target_pairs={{0,56},{8,0},{16,8},{24,16},{32,24},{40,32},{48,40},{56,48},{1,57}... | collective-permute-start | bytes 417800 | tf_op jit(solution)/shard_map/ppermute | solution.py:320
  58.0 5.0 %shard_map.77.acc_in = f32[4,272,1024]{2,1,0:T(8,128)S(1)} custom-call(bf16[4,272,256]{2,1,0:T(8,128)(2,1)S(1)} %get-tuple-element.41.h, bf16[4608,1024]{1,0:T(8,128)(2,1)S(1)} %bitcast.7, f32[4,272,1024]{2,1,0:T(8,128)S(1)} %get-tuple-element.42.acc_in), custom_call_target="tpu_custom_call", output_to_operand_aliasing={{}: (2, {})} | custom-call | flops 4348654592 | bytes 1048576 | tf_op jit(solution)/shard_map/pallas_call | solution.py:30
  63.0 0.0 collective-permute-done.8.bot
  63.0 1.4 %shard_map.78 = (f32[4,272,1024]{2,1,0:T(8,128)S(1)}, bf16[2,272,256]{2,1,0:T(8,128)(2,1)S(1)}) custom-call(bf16[272,256]{1,0:T(8,128)(2,1)S(1)} %collective-permute-done.7.top, bf16[272,256]{1,0:T(8,128)(2,1)S(1)} %collective-permute-done.8.bot, bf16[4608,1024]{1,0:T(8,128)(2,1)S(1)} %bitcast.8, ...), custom_call_target="tpu_custom_call", output_to_operand_aliasing={{0}: (3, {})} | custom-call | flops 966367616 | bytes 1048576 | tf_op jit(solution)/shard_map/pallas_call | solution.py:30
  64.4 0.1 collective-permute-start.9
  64.5 5.0 %shard_map.79.acc_in = f32[4,272,1024]{2,1,0:T(8,128)S(1)} custom-call(bf16[4,272,256]{2,1,0:T(8,128)(2,1)S(1)} %collective-permute-done.10.recv, bf16[4608,1024]{1,0:T(8,128)(2,1)S(1)} %bitcast.9, f32[4,272,1024]{2,1,0:T(8,128)S(1)} %get-tuple-element.45.acc_in), custom_call_target="tpu_custom_call", output_to_operand_aliasing={{}: (2, {})} | custom-call | flops 4348654592 | bytes 1048576 | tf_op jit(solution)/shard_map/pallas_call | solution.py:30
  69.5 3.5 %shard_map.80 = (f32[4,272,1024]{2,1,0:T(8,128)S(1)}, bf16[1,4,256,256]{3,2,1,0:T(8,128)(2,1)}, f32[1,4,256,256]{3,2,1,0:T(8,128)}) custom-call(bf16[2,272,256]{2,1,0:T(8,128)(2,1)S(1)} %collective-permute-done.9.two, bf16[4,272,256]{2,1,0:T(8,128)(2,1)S(1)} %get-tuple-element.41.h, ...), custom_call_target="tpu_custom_call", output_to_operand_aliasing={{0}: (5, {})} | custom-call | flops 2899102976 | bytes 1048576 | tf_op jit(solution)/shard_map/pallas_call | solution.py:30
  (23 shorter events, 0.1 us)
Async XLA Ops:
  0.6 1.0 %copy-start.2 = (bf16[1,4,256,256]{3,2,1,0:T(8,128)(2,1)S(1)}, bf16[1,4,256,256]{3,2,1,0:T(8,128)(2,1)}, u32[]{:S(2)}) copy-start(bf16[1,4,256,256]{3,2,1,0:T(8,128)(2,1)} %hid.7) | copy-start | bytes 1572868
  1.7 1.2 %copy-start.5 = (bf16[2,4,256,256]{3,2,1,0:T(8,128)(2,1)S(1)}, bf16[2,4,256,256]{3,2,1,0:T(8,128)(2,1)}, u32[]{:S(2)}) copy-start(bf16[2,4,256,256]{3,2,1,0:T(8,128)(2,1)} %fr.5) | copy-start | bytes 3145732
  2.9 1.2 %copy-start.7 = (f32[1,4,256,256]{3,2,1,0:T(8,128)S(1)}, f32[1,4,256,256]{3,2,1,0:T(8,128)}, u32[]{:S(2)}) copy-start(f32[1,4,256,256]{3,2,1,0:T(8,128)} %cell.3) | copy-start | bytes 3145732
  4.1 15.3 %collective-permute-start = (bf16[20,8,256]{2,1,0:T(8,128)(2,1)S(1)}, bf16[20,8,256]{2,1,0:T(8,128)(2,1)S(1)}, u32[]{:S(2)}, u32[]{:S(2)}) collective-permute-start(bf16[20,8,256]{2,1,0:T(8,128)(2,1)S(1)} %get-tuple-element.25), channel_id=1, source_target_pairs={{0,1},{1,2},{2,3},{3,4},{4,5},{5,6},{6,7},{7,0},{8,9},{9,10},{10,1... | collective-permute-start | bytes 245768 | tf_op jit(solution)/shard_map/ppermute | solution.py:319
  8.0 11.5 %collective-permute-start.1 = (bf16[20,8,256]{2,1,0:T(8,128)(2,1)S(1)}, bf16[20,8,256]{2,1,0:T(8,128)(2,1)S(1)}, u32[]{:S(2)}, u32[]{:S(2)}) collective-permute-start(bf16[20,8,256]{2,1,0:T(8,128)(2,1)S(1)} %get-tuple-element.26), channel_id=1, source_target_pairs={{0,7},{1,0},{2,1},{3,2},{4,3},{5,4},{6,5},{7,6},{8,15},{9,8},{10,9... | collective-permute-start | bytes 245768 | tf_op jit(solution)/shard_map/ppermute | solution.py:320
  10.2 3.7 %copy-start = (bf16[1,4608,1024]{2,1,0:T(8,128)(2,1)S(1)}, bf16[1,4608,1024]{2,1,0:T(8,128)(2,1)}, u32[]{:S(2)}) copy-start(bf16[1,4608,1024]{2,1,0:T(8,128)(2,1)} %param.8) | copy-start | bytes 28311556
  13.9 1.0 %copy-start.3 = (bf16[1,4,256,256]{3,2,1,0:T(8,128)(2,1)S(1)}, bf16[1,4,256,256]{3,2,1,0:T(8,128)(2,1)}, u32[]{:S(2)}) copy-start(bf16[1,4,256,256]{3,2,1,0:T(8,128)(2,1)} %hid.7) | copy-start | bytes 1572868
  15.0 4.5 %copy-start.4 = (bf16[1,4,256,256]{3,2,1,0:T(8,128)(2,1)S(1)}, bf16[1,4,256,256]{3,2,1,0:T(8,128)(2,1)}, u32[]{:S(2)}) copy-start(bf16[1,4,256,256]{3,2,1,0:T(8,128)(2,1)} %hid.7) | copy-start | bytes 1572868
  15.0 4.5 %copy-start.6 = (bf16[2,4,256,256]{3,2,1,0:T(8,128)(2,1)S(1)}, bf16[2,4,256,256]{3,2,1,0:T(8,128)(2,1)}, u32[]{:S(2)}) copy-start(bf16[2,4,256,256]{3,2,1,0:T(8,128)(2,1)} %fr.5) | copy-start | bytes 3145732
  15.0 9.4 %copy-start.1 = (bf16[1,4608,1024]{2,1,0:T(8,128)(2,1)S(1)}, bf16[1,4608,1024]{2,1,0:T(8,128)(2,1)}, u32[]{:S(2)}) copy-start(bf16[1,4608,1024]{2,1,0:T(8,128)(2,1)} %param.8) | copy-start | bytes 28311556
  15.0 9.4 %copy-start.8 = (f32[1,4,256,256]{3,2,1,0:T(8,128)S(1)}, f32[1,4,256,256]{3,2,1,0:T(8,128)}, u32[]{:S(2)}) copy-start(f32[1,4,256,256]{3,2,1,0:T(8,128)} %cell.3) | copy-start | bytes 3145732
  19.5 13.5 %collective-permute-start.2 = (bf16[3,272,256]{2,1,0:T(8,128)(2,1)S(1)}, bf16[3,272,256]{2,1,0:T(8,128)(2,1)S(1)}, u32[]{:S(2)}, u32[]{:S(2)}) collective-permute-start(bf16[3,272,256]{2,1,0:T(8,128)(2,1)S(1)} %get-tuple-element.27), channel_id=1, source_target_pairs={{0,8},{8,16},{16,24},{24,32},{32,40},{40,48},{48,56},{56,0},{1,9},... | collective-permute-start | bytes 1253384 | tf_op jit(solution)/shard_map/ppermute | solution.py:319
  21.2 11.8 %copy-start.9 = (f32[2,1024]{1,0:T(2,128)S(1)}, f32[2,1024]{1,0:T(2,128)}, u32[]{:S(2)}) copy-start(f32[2,1024]{1,0:T(2,128)} %bias.5) | copy-start | bytes 24580
  21.2 11.7 %collective-permute-start.3 = (bf16[3,272,256]{2,1,0:T(8,128)(2,1)S(1)}, bf16[3,272,256]{2,1,0:T(8,128)(2,1)S(1)}, u32[]{:S(2)}, u32[]{:S(2)}) collective-permute-start(bf16[3,272,256]{2,1,0:T(8,128)(2,1)S(1)} %get-tuple-element.28), channel_id=1, source_target_pairs={{0,56},{8,0},{16,8},{24,16},{32,24},{40,32},{48,40},{56,48},{1,57}... | collective-permute-start | bytes 1253384 | tf_op jit(solution)/shard_map/ppermute | solution.py:320
  34.3 7.8 %collective-permute-start.4 = (bf16[4,272,256]{2,1,0:T(8,128)(2,1)S(1)}, bf16[4,272,256]{2,1,0:T(8,128)(2,1)S(1)}, u32[]{:S(2)}, u32[]{:S(2)}) collective-permute-start(bf16[4,272,256]{2,1,0:T(8,128)(2,1)S(1)} %get-tuple-element.31.h), channel_id=1, source_target_pairs={{0,64},{64,0},{1,65},{65,1},{2,66},{66,2},{3,67},{67,3},{4,68},{68... | collective-permute-start | bytes 1671176 | tf_op jit(solution)/shard_map/ppermute | solution.py:354
  42.2 8.6 %collective-permute-start.5 = (bf16[272,256]{1,0:T(8,128)(2,1)S(1)}, bf16[272,256]{1,0:T(8,128)(2,1)S(1)}, u32[]{:S(2)}, u32[]{:S(2)}) collective-permute-start(bf16[272,256]{1,0:T(8,128)(2,1)S(1)} %get-tuple-element.32), channel_id=1, source_target_pairs={{0,8},{8,16},{16,24},{24,32},{32,40},{40,48},{48,56},{56,0},{1,9},... | collective-permute-start | bytes 417800 | tf_op jit(solution)/shard_map/ppermute | solution.py:319
  42.3 8.6 %collective-permute-start.6 = (bf16[272,256]{1,0:T(8,128)(2,1)S(1)}, bf16[272,256]{1,0:T(8,128)(2,1)S(1)}, u32[]{:S(2)}, u32[]{:S(2)}) collective-permute-start(bf16[272,256]{1,0:T(8,128)(2,1)S(1)} %get-tuple-element.33), channel_id=1, source_target_pairs={{0,56},{8,0},{16,8},{24,16},{32,24},{40,32},{48,40},{56,48},{1,57}... | collective-permute-start | bytes 417800 | tf_op jit(solution)/shard_map/ppermute | solution.py:320
  53.4 11.1 %collective-permute-start.10 = (bf16[4,272,256]{2,1,0:T(8,128)(2,1)S(1)}, bf16[4,272,256]{2,1,0:T(8,128)(2,1)S(1)}, u32[]{:S(2)}, u32[]{:S(2)}) collective-permute-start(bf16[4,272,256]{2,1,0:T(8,128)(2,1)S(1)} %get-tuple-element.41.h), channel_id=1, source_target_pairs={{0,64},{64,0},{1,65},{65,1},{2,66},{66,2},{3,67},{67,3},{4,68},{68... | collective-permute-start | bytes 1671176 | tf_op jit(solution)/shard_map/ppermute | solution.py:379
  54.4 8.6 %collective-permute-start.7 = (bf16[272,256]{1,0:T(8,128)(2,1)S(1)}, bf16[272,256]{1,0:T(8,128)(2,1)S(1)}, u32[]{:S(2)}, u32[]{:S(2)}) collective-permute-start(bf16[272,256]{1,0:T(8,128)(2,1)S(1)} %get-tuple-element.39), channel_id=1, source_target_pairs={{0,8},{8,16},{16,24},{24,32},{32,40},{40,48},{48,56},{56,0},{1,9},... | collective-permute-start | bytes 417800 | tf_op jit(solution)/shard_map/ppermute | solution.py:319
  54.4 8.6 %collective-permute-start.8 = (bf16[272,256]{1,0:T(8,128)(2,1)S(1)}, bf16[272,256]{1,0:T(8,128)(2,1)S(1)}, u32[]{:S(2)}, u32[]{:S(2)}) collective-permute-start(bf16[272,256]{1,0:T(8,128)(2,1)S(1)} %get-tuple-element.40), channel_id=1, source_target_pairs={{0,56},{8,0},{16,8},{24,16},{32,24},{40,32},{48,40},{56,48},{1,57}... | collective-permute-start | bytes 417800 | tf_op jit(solution)/shard_map/ppermute | solution.py:320
  64.4 5.1 %collective-permute-start.9 = (bf16[2,272,256]{2,1,0:T(8,128)(2,1)S(1)}, bf16[2,272,256]{2,1,0:T(8,128)(2,1)S(1)}, u32[]{:S(2)}, u32[]{:S(2)}) collective-permute-start(bf16[2,272,256]{2,1,0:T(8,128)(2,1)S(1)} %get-tuple-element.43), channel_id=1, source_target_pairs={{0,64},{64,0},{1,65},{65,1},{2,66},{66,2},{3,67},{67,3},{4,68},{68... | collective-permute-start | bytes 835592 | tf_op jit(solution)/shard_map/ppermute | solution.py:391
